TPU v7x, 256 devices: a whole 4x4x8 slice. The times are simulated.
256 devices in a mesh: outer: 16 (over y, z_hi), inner: 16 (over x, z_lo, core).
Axes of the slice: x: 4, y: 4, z: 8 (z_hi: 4, z_lo: 2; z = z_hi * 2 + z_lo), core: 2. Of those that a mesh axis runs over, the one named last changes fastest.
Arguments:
- hidden: bfloat16 [32768, 1024], P(('outer', 'inner')), may hold values from -24 to 24
- x_act: bfloat16 [32768, 2048], P(('outer', 'inner')), may hold values from -6 to 6
- dt_step: float32 [32768, 32], P(('outer', 'inner')), may hold values from 0.0014915534 to 0.44, as said below
- log_decay: float32 [32768, 32], P(('outer', 'inner')), may hold values from -0.81 to -8.85009766e-07, as said below
- w_bc: bfloat16 [1024, 128], P(('outer', 'inner')), may hold values from -0.1875 to 0.1875
- grad_y: bfloat16 [32768, 2048], P(('outer', 'inner')), may hold values from -0.19921875 to 0.19921875
Outputs:
- grad_x: float32 [32768, 2048], P(('outer', 'inner'))
- grad_hidden: float32 [32768, 1024], P(('outer', 'inner'))
- grad_proj: float32 [1024, 128], P(('outer', 'inner'))
Inputs may be any that keep to these rules, and one draw needn't show every extreme that they name: `dt_step`: Positive; constant in scale within each head apart from a factor within e**-0.5 to e**0.5. `log_decay`: Negative.
All inputs are finite; a program needn't handle non-finite values.
Results may differ from a plain program's by a relative error of at most 0.0029.
Values may be sent and summed in bfloat16 or wider, within the bound.
A program may use at most 64 MiB of HBM per device.

v0:
```python
import math

import jax
import jax.numpy as jnp
from jax import lax
from jax.sharding import PartitionSpec as P

BLOCK = 128


HIGH = lax.Precision.HIGHEST


def shifted(value, axis, steps):
    count = lax.axis_size(axis)
    first, last = (max(0, -steps), min(count, count - steps))
    return lax.ppermute(value, axis, [(source, source + steps) for source in range(first, last)])


def block_step(carried, pieces):
    inputs, decays, b_rows, c_rows = pieces
    length = inputs.shape[0]
    running = jnp.cumsum(decays, axis=0)
    row_ids = lax.broadcasted_iota(jnp.int32, (length, length), 0)
    col_ids = lax.broadcasted_iota(jnp.int32, (length, length), 1)
    causal = row_ids >= col_ids
    spread = running.T[:, :, None] - running.T[:, None, :]
    segment = jnp.where(causal[None], jnp.exp(jnp.where(causal[None], spread, 0.0)), 0.0)
    scores = jnp.einsum("in,jn->ij", c_rows, b_rows, precision=HIGH)
    outputs = jnp.einsum("hij,jhp->ihp", segment * scores[None], inputs, precision=HIGH)
    outputs = outputs + jnp.exp(running)[:, :, None] * jnp.einsum(
        "in,hpn->ihp", c_rows, carried, precision=HIGH
    )
    final_sum = running[-1]
    weights = jnp.exp(final_sum[None, :] - running)
    updated = jnp.exp(final_sum)[:, None, None] * carried + jnp.einsum(
        "jhp,jn->hpn", inputs * weights[:, :, None], b_rows, precision=HIGH
    )
    return (updated, outputs)


def scan_block(inputs, decays, b_rows, c_rows, carried, length):
    count = inputs.shape[0] // length
    pieces = (
        inputs.reshape((count, length) + inputs.shape[1:]),
        decays.reshape((count, length, decays.shape[1])),
        b_rows.reshape((count, length, b_rows.shape[1])),
        c_rows.reshape((count, length, c_rows.shape[1])),
    )
    final_state, outputs = lax.scan(block_step, carried, pieces)
    return (outputs.reshape(inputs.shape), final_state)


def combine(earlier, later):
    return (earlier[0] + later[0], jnp.exp(later[0])[:, None, None] * earlier[1] + later[1])


def doubling_prefix(own, backward):
    device_count = lax.axis_size(("outer", "inner"))
    distances = [1]
    reach = 1
    while reach < device_count:
        distances.append(reach)
        reach = reach * 2
    gathered = own
    for number, distance in enumerate(distances):
        if backward:
            arrived = shifted((gathered[0], gathered[1]), ("outer", "inner"), -distance)
        else:
            arrived = shifted((gathered[0], gathered[1]), ("outer", "inner"), distance)
        if number == 0:
            gathered = arrived
        else:
            gathered = combine(arrived, gathered)
    return gathered


def per_device(hidden, x_act, dt_step, log_decay, w_bc, grad_y):
    weights_full = lax.all_gather(w_bc, ("outer", "inner"), axis=0, tiled=True)
    state_width = weights_full.shape[1] // 2
    row_count = hidden.shape[0]
    head_count = dt_step.shape[1]
    head_size = x_act.shape[1] // head_count
    projected = jnp.dot(hidden, weights_full, preferred_element_type=jnp.float32)
    b_rows = projected[:, :state_width]
    c_rows = projected[:, state_width:]
    inputs = dt_step[:, :, None] * x_act.astype(jnp.float32).reshape(
        row_count, head_count, head_size
    )
    cotangent = grad_y.astype(jnp.float32).reshape(row_count, head_count, head_size)
    running = jnp.cumsum(log_decay, axis=0)
    totals = running[-1]
    own_state = jnp.einsum(
        "jhp,jn->hpn",
        inputs * jnp.exp(totals[None, :] - running)[:, :, None],
        b_rows,
        precision=HIGH,
    )
    own_adjoint = jnp.einsum(
        "ihp,in->hpn", cotangent * jnp.exp(running)[:, :, None], c_rows, precision=HIGH
    )
    state_in = doubling_prefix((totals, own_state), False)[1]
    adjoint_out = doubling_prefix((totals, own_adjoint), True)[1]

    def forward(inputs, b_rows, c_rows):
        return scan_block(inputs, log_decay, b_rows, c_rows, state_in, BLOCK)

    outputs, pullback = jax.vjp(forward, inputs, b_rows, c_rows)
    d_in, d_b, d_c = pullback((cotangent, adjoint_out))
    grad_x = (dt_step[:, :, None] * d_in).reshape(row_count, head_count * head_size)
    d_proj = jnp.concatenate([d_b, d_c], axis=1)
    d_low = d_proj.astype(jnp.bfloat16)
    grad_hidden = lax.dot_general(
        d_low, weights_full, (((1,), (1,)), ((), ())), preferred_element_type=jnp.float32
    )
    scale = 1.0 / math.sqrt(row_count * lax.axis_size("outer") * lax.axis_size("inner"))
    grad_proj = lax.psum_scatter(
        lax.dot_general(hidden, d_low, (((0,), (0,)), ((), ())), preferred_element_type=jnp.float32)
        * scale,
        ("outer", "inner"),
        scatter_dimension=0,
        tiled=True,
    )
    return (grad_x, grad_hidden, grad_proj)


def solution(mesh):
    in_specs = (
        P(("outer", "inner"), None),
        P(("outer", "inner"), None),
        P(("outer", "inner"), None),
        P(("outer", "inner"), None),
        P(("outer", "inner"), None),
        P(("outer", "inner"), None),
    )
    out_specs = (
        P(("outer", "inner"), None),
        P(("outer", "inner"), None),
        P(("outer", "inner"), None),
    )
    return jax.shard_map(
        per_device, mesh=mesh, in_specs=in_specs, out_specs=out_specs, check_vma=False
    )
```

profile of v0, /device:TPU:1, one launch (start us, length us, event | category | flops | bytes accessed | tf_op | source)
XLA Modules:
  0.0 1106.5 jit_solution(5641933597297097670)
XLA Ops:
  8.3 5.1 collective-permute-start
  15.5 348.4 %all-gather = bf16[256,4,128]{2,1,0:T(4,128)(2,1)S(1)} all-gather(bf16[1,4,128]{2,1,0:T(4,128)(2,1)} %bitcast.65), channel_id=1, replica_groups=mesh['outer'=16,'inner'=16] {'outer','inner'}, dimensions={0}, use_global_device_ids=true | all-gather | bytes 263168 | tf_op jit(solution)/shard_map/all_gather | solution.py:79
  379.3 3.5 fusion.3
  384.7 3.6 collective-permute-start.18
  388.4 5.6 collective-permute-done.1
  395.3 4.0 collective-permute-start.19
  400.7 4.0 collective-permute-start.20
  409.1 5.5 collective-permute-start.21
  419.1 3.9 collective-permute-done.9
  425.7 3.8 collective-permute-done.26
  429.7 9.5 collective-permute-start.27
  440.5 41.9 %collective-permute-done.10 = f32[32,64,64]{2,1,0:T(8,128)S(1)} collective-permute-done((f32[32,64,64]{2,1,0:T(8,128)S(1)}, f32[32,64,64]{2,1,0:T(8,128)S(1)}, u32[]{:S(2)}, u32[]{:S(2)}) %collective-permute-start.10) | collective-permute-done | bytes 524320 | tf_op jit(solution)/shard_map/ppermute | solution.py:17
  484.1 19.0 %collective-permute-start.28 = (f32[32,64,64]{2,1,0:T(8,128)S(1)}, f32[32,64,64]{2,1,0:T(8,128)S(1)}, u32[]{:S(2)}, u32[]{:S(2)}) collective-permute-start(f32[32,64,64]{2,1,0:T(8,128)S(1)} %multiply_add_fusion.5), channel_id=1, source_target_pairs={{0,4},{1,5},{2,6},{3,7},{4,8},{5,9},{6,10},{7,11},{8,12},{9,13},{1... | collective-permute-start | bytes 1572872 | tf_op jit(solution)/shard_map/ppermute | solution.py:17
  505.9 20.1 %collective-permute-done.28 = f32[32,64,64]{2,1,0:T(8,128)S(1)} collective-permute-done((f32[32,64,64]{2,1,0:T(8,128)S(1)}, f32[32,64,64]{2,1,0:T(8,128)S(1)}, u32[]{:S(2)}, u32[]{:S(2)}) %collective-permute-start.28) | collective-permute-done | bytes 524320 | tf_op jit(solution)/shard_map/ppermute | solution.py:17
  530.6 21.1 %collective-permute-done.12 = f32[32,64,64]{2,1,0:T(8,128)S(1)} collective-permute-done((f32[32,64,64]{2,1,0:T(8,128)S(1)}, f32[32,64,64]{2,1,0:T(8,128)S(1)}, u32[]{:S(2)}, u32[]{:S(2)}) %collective-permute-start.12) | collective-permute-done | bytes 524320 | tf_op jit(solution)/shard_map/ppermute | solution.py:17
  553.4 13.6 %collective-permute-done.29 = f32[32,64,64]{2,1,0:T(8,128)S(1)} collective-permute-done((f32[32,64,64]{2,1,0:T(8,128)S(1)}, f32[32,64,64]{2,1,0:T(8,128)S(1)}, u32[]{:S(2)}, u32[]{:S(2)}) %collective-permute-start.29) | collective-permute-done | bytes 524320 | tf_op jit(solution)/shard_map/ppermute | solution.py:17
  567.2 56.7 %collective-permute-start.30 = (f32[32,64,64]{2,1,0:T(8,128)S(1)}, f32[32,64,64]{2,1,0:T(8,128)S(1)}, u32[]{:S(2)}, u32[]{:S(2)}) collective-permute-start(f32[32,64,64]{2,1,0:T(8,128)S(1)} %multiply_add_fusion.3), channel_id=1, source_target_pairs={{0,16},{1,17},{2,18},{3,19},{4,20},{5,21},{6,22},{7,23},{8,24},{9,... | collective-permute-start | bytes 1572872 | tf_op jit(solution)/shard_map/ppermute | solution.py:17
  626.7 8.9 collective-permute-done.30
  635.8 7.9 collective-permute-start.31
  643.7 67.7 %collective-permute-start.24 = (f32[32]{0:T(128)S(1)}, f32[32]{0:T(128)S(1)}, u32[]{:S(2)}, u32[]{:S(2)}) collective-permute-start(f32[32]{0:T(128)S(1)} %get-tuple-element.170), channel_id=1, source_target_pairs={{0,64},{1,65},{2,66},{3,67},{4,68},{5,69},{6,70},{7,71},{8,72},{9,... | collective-permute-start | bytes 392 | tf_op jit(solution)/shard_map/ppermute | solution.py:17
  713.1 44.7 %collective-permute-start.32 = (f32[32,64,64]{2,1,0:T(8,128)S(1)}, f32[32,64,64]{2,1,0:T(8,128)S(1)}, u32[]{:S(2)}, u32[]{:S(2)}) collective-permute-start(f32[32,64,64]{2,1,0:T(8,128)S(1)} %multiply_add_fusion.1), channel_id=1, source_target_pairs={{0,64},{1,65},{2,66},{3,67},{4,68},{5,69},{6,70},{7,71},{8,72},{9,... | collective-permute-start | bytes 1572872 | tf_op jit(solution)/shard_map/ppermute | solution.py:17
  759.3 19.4 %collective-permute-done.32 = f32[32,64,64]{2,1,0:T(8,128)S(1)} collective-permute-done((f32[32,64,64]{2,1,0:T(8,128)S(1)}, f32[32,64,64]{2,1,0:T(8,128)S(1)}, u32[]{:S(2)}, u32[]{:S(2)}) %collective-permute-start.32) | collective-permute-done | bytes 524320 | tf_op jit(solution)/shard_map/ppermute | solution.py:17
  782.3 9.6 collective-permute-done.33
  799.7 298.4 %all-reduce.3.cloned.1.call-done = f32[1024,128]{0,1:T(8,128)} async-done(((f32[1024,128]{0,1:T(8,128)}), f32[1024,128]{0,1:T(8,128)}) %all-reduce.3.cloned.1.call-update) | async-done | bytes 524304
  (123 shorter events, 65.5 us)
Async XLA Ops:
  7.2 1090.9 %all-reduce.3.cloned.1.call-start = ((), (), s32[]{:S(2)}) async-start(), calls=%async_computation | async-start | bytes 1048576
  8.3 374.5 %collective-permute-start = (f32[32]{0:T(128)S(1)}, f32[32]{0:T(128)S(1)}, u32[]{:S(2)}, u32[]{:S(2)}) collective-permute-start(f32[32]{0:T(128)S(1)} %slice_bitcast_fusion), channel_id=1, source_target_pairs={{1,0},{2,1},{3,2},{4,3},{5,4},{6,5},{7,6},{8,7},{9,8},{10,9},{11,1... | collective-permute-start | bytes 392 | tf_op jit(solution)/shard_map/ppermute | solution.py:17
  13.5 371.3 %collective-permute-start.17 = (f32[32]{0:T(128)S(1)}, f32[32]{0:T(128)S(1)}, u32[]{:S(2)}, u32[]{:S(2)}) collective-permute-start(f32[32]{0:T(128)S(1)} %slice_bitcast_fusion), channel_id=1, source_target_pairs={{0,1},{1,2},{2,3},{3,4},{4,5},{5,6},{6,7},{7,8},{8,9},{9,10},{10,1... | collective-permute-start | bytes 392 | tf_op jit(solution)/shard_map/ppermute | solution.py:17
  366.4 38.2 %collective-permute-start.8 = (f32[32,64,64]{2,1,0:T(8,128)}, f32[32,64,64]{2,1,0:T(8,128)}, u32[]{:S(2)}, u32[]{:S(2)}) collective-permute-start(f32[32,64,64]{2,1,0:T(8,128)} %fusion.19), channel_id=1, source_target_pairs={{1,0},{2,1},{3,2},{4,3},{5,4},{6,5},{7,6},{8,7},{9,8},{10,9},{11,1... | collective-permute-start | bytes 1572872 | tf_op jit(solution)/shard_map/ppermute | solution.py:17
  370.9 43.7 %collective-permute-start.25 = (f32[32,64,64]{2,1,0:T(8,128)}, f32[32,64,64]{2,1,0:T(8,128)S(1)}, u32[]{:S(2)}, u32[]{:S(2)}) collective-permute-start(f32[32,64,64]{2,1,0:T(8,128)} %fusion.22), channel_id=1, source_target_pairs={{0,1},{1,2},{2,3},{3,4},{4,5},{5,6},{6,7},{7,8},{8,9},{9,10},{10,1... | collective-permute-start | bytes 1572872 | tf_op jit(solution)/shard_map/ppermute | solution.py:17
  409.1 30.1 %collective-permute-start.21 = (f32[32]{0:T(128)S(1)}, f32[32]{0:T(128)S(1)}, u32[]{:S(2)}, u32[]{:S(2)}) collective-permute-start(f32[32]{0:T(128)S(1)} %get-tuple-element.176), channel_id=1, source_target_pairs={{0,8},{1,9},{2,10},{3,11},{4,12},{5,13},{6,14},{7,15},{8,16},{9,17... | collective-permute-start | bytes 392 | tf_op jit(solution)/shard_map/ppermute | solution.py:17
  417.8 85.3 %collective-permute-start.5 = (f32[32]{0:T(128)S(1)}, f32[32]{0:T(128)S(1)}, u32[]{:S(2)}, u32[]{:S(2)}) collective-permute-start(f32[32]{0:T(128)S(1)} %get-tuple-element.186), channel_id=1, source_target_pairs={{16,0},{17,1},{18,2},{19,3},{20,4},{21,5},{22,6},{23,7},{24,8},{25... | collective-permute-start | bytes 392 | tf_op jit(solution)/shard_map/ppermute | solution.py:17
  424.4 58.0 %collective-permute-start.10 = (f32[32,64,64]{2,1,0:T(8,128)S(1)}, f32[32,64,64]{2,1,0:T(8,128)S(1)}, u32[]{:S(2)}, u32[]{:S(2)}) collective-permute-start(f32[32,64,64]{2,1,0:T(8,128)S(1)} %multiply_add_fusion.14), channel_id=1, source_target_pairs={{2,0},{3,1},{4,2},{5,3},{6,4},{7,5},{8,6},{9,7},{10,8},{11,9},{12,... | collective-permute-start | bytes 1572872 | tf_op jit(solution)/shard_map/ppermute | solution.py:17
  429.7 54.2 %collective-permute-start.27 = (f32[32,64,64]{2,1,0:T(8,128)S(1)}, f32[32,64,64]{2,1,0:T(8,128)S(1)}, u32[]{:S(2)}, u32[]{:S(2)}) collective-permute-start(f32[32,64,64]{2,1,0:T(8,128)S(1)} %multiply_add_fusion.6), channel_id=1, source_target_pairs={{0,2},{1,3},{2,4},{3,5},{4,6},{5,7},{6,8},{7,9},{8,10},{9,11},{10,... | collective-permute-start | bytes 1572872 | tf_op jit(solution)/shard_map/ppermute | solution.py:17
  439.2 90.1 %collective-permute-start.22 = (f32[32]{0:T(128)S(1)}, f32[32]{0:T(128)S(1)}, u32[]{:S(2)}, u32[]{:S(2)}) collective-permute-start(f32[32]{0:T(128)S(1)} %get-tuple-element.174), channel_id=1, source_target_pairs={{0,16},{1,17},{2,18},{3,19},{4,20},{5,21},{6,22},{7,23},{8,24},{9,... | collective-permute-start | bytes 392 | tf_op jit(solution)/shard_map/ppermute | solution.py:17
  484.1 42.0 %collective-permute-start.28 = (f32[32,64,64]{2,1,0:T(8,128)S(1)}, f32[32,64,64]{2,1,0:T(8,128)S(1)}, u32[]{:S(2)}, u32[]{:S(2)}) collective-permute-start(f32[32,64,64]{2,1,0:T(8,128)S(1)} %multiply_add_fusion.5), channel_id=1, source_target_pairs={{0,4},{1,5},{2,6},{3,7},{4,8},{5,9},{6,10},{7,11},{8,12},{9,13},{1... | collective-permute-start | bytes 1572872 | tf_op jit(solution)/shard_map/ppermute | solution.py:17
  503.1 120.8 %collective-permute-start.6 = (f32[32]{0:T(128)S(1)}, f32[32]{0:T(128)S(1)}, u32[]{:S(2)}, u32[]{:S(2)}) collective-permute-start(f32[32]{0:T(128)S(1)} %get-tuple-element.184), channel_id=1, source_target_pairs={{32,0},{33,1},{34,2},{35,3},{36,4},{37,5},{38,6},{39,7},{40,8},{41... | collective-permute-start | bytes 392 | tf_op jit(solution)/shard_map/ppermute | solution.py:17
  504.6 47.1 %collective-permute-start.12 = (f32[32,64,64]{2,1,0:T(8,128)S(1)}, f32[32,64,64]{2,1,0:T(8,128)S(1)}, u32[]{:S(2)}, u32[]{:S(2)}) collective-permute-start(f32[32,64,64]{2,1,0:T(8,128)S(1)} %multiply_add_fusion.12), channel_id=1, source_target_pairs={{8,0},{9,1},{10,2},{11,3},{12,4},{13,5},{14,6},{15,7},{16,8},{17,9... | collective-permute-start | bytes 1572872 | tf_op jit(solution)/shard_map/ppermute | solution.py:17
  526.2 40.8 %collective-permute-start.29 = (f32[32,64,64]{2,1,0:T(8,128)S(1)}, f32[32,64,64]{2,1,0:T(8,128)S(1)}, u32[]{:S(2)}, u32[]{:S(2)}) collective-permute-start(f32[32,64,64]{2,1,0:T(8,128)S(1)} %multiply_add_fusion.4), channel_id=1, source_target_pairs={{0,8},{1,9},{2,10},{3,11},{4,12},{5,13},{6,14},{7,15},{8,16},{9,17... | collective-permute-start | bytes 1572872 | tf_op jit(solution)/shard_map/ppermute | solution.py:17
  529.3 114.4 %collective-permute-start.23 = (f32[32]{0:T(128)S(1)}, f32[32]{0:T(128)S(1)}, u32[]{:S(2)}, u32[]{:S(2)}) collective-permute-start(f32[32]{0:T(128)S(1)} %get-tuple-element.172), channel_id=1, source_target_pairs={{0,32},{1,33},{2,34},{3,35},{4,36},{5,37},{6,38},{7,39},{8,40},{9,... | collective-permute-start | bytes 392 | tf_op jit(solution)/shard_map/ppermute | solution.py:17
  551.9 73.4 %collective-permute-start.13 = (f32[32,64,64]{2,1,0:T(8,128)S(1)}, f32[32,64,64]{2,1,0:T(8,128)S(1)}, u32[]{:S(2)}, u32[]{:S(2)}) collective-permute-start(f32[32,64,64]{2,1,0:T(8,128)S(1)} %multiply_add_fusion.11), channel_id=1, source_target_pairs={{16,0},{17,1},{18,2},{19,3},{20,4},{21,5},{22,6},{23,7},{24,8},{25... | collective-permute-start | bytes 1572872 | tf_op jit(solution)/shard_map/ppermute | solution.py:17
  567.2 68.5 %collective-permute-start.30 = (f32[32,64,64]{2,1,0:T(8,128)S(1)}, f32[32,64,64]{2,1,0:T(8,128)S(1)}, u32[]{:S(2)}, u32[]{:S(2)}) collective-permute-start(f32[32,64,64]{2,1,0:T(8,128)S(1)} %multiply_add_fusion.3), channel_id=1, source_target_pairs={{0,16},{1,17},{2,18},{3,19},{4,20},{5,21},{6,22},{7,23},{8,24},{9,... | collective-permute-start | bytes 1572872 | tf_op jit(solution)/shard_map/ppermute | solution.py:17
  624.0 133.9 %collective-permute-start.7 = (f32[32]{0:T(128)S(1)}, f32[32]{0:T(128)S(1)}, u32[]{:S(2)}, u32[]{:S(2)}) collective-permute-start(f32[32]{0:T(128)S(1)} %get-tuple-element.182), channel_id=1, source_target_pairs={{64,0},{65,1},{66,2},{67,3},{68,4},{69,5},{70,6},{71,7},{72,8},{73... | collective-permute-start | bytes 392 | tf_op jit(solution)/shard_map/ppermute | solution.py:17
  625.4 86.0 %collective-permute-start.14 = (f32[32,64,64]{2,1,0:T(8,128)S(1)}, f32[32,64,64]{2,1,0:T(8,128)S(1)}, u32[]{:S(2)}, u32[]{:S(2)}) collective-permute-start(f32[32,64,64]{2,1,0:T(8,128)S(1)} %multiply_add_fusion.10), channel_id=1, source_target_pairs={{32,0},{33,1},{34,2},{35,3},{36,4},{37,5},{38,6},{39,7},{40,8},{41... | collective-permute-start | bytes 1572872 | tf_op jit(solution)/shard_map/ppermute | solution.py:17
  635.8 77.1 %collective-permute-start.31 = (f32[32,64,64]{2,1,0:T(8,128)S(1)}, f32[32,64,64]{2,1,0:T(8,128)S(1)}, u32[]{:S(2)}, u32[]{:S(2)}) collective-permute-start(f32[32,64,64]{2,1,0:T(8,128)S(1)} %multiply_add_fusion.2), channel_id=1, source_target_pairs={{0,32},{1,33},{2,34},{3,35},{4,36},{5,37},{6,38},{7,39},{8,40},{9,... | collective-permute-start | bytes 1572872 | tf_op jit(solution)/shard_map/ppermute | solution.py:17
  643.7 136.5 %collective-permute-start.24 = (f32[32]{0:T(128)S(1)}, f32[32]{0:T(128)S(1)}, u32[]{:S(2)}, u32[]{:S(2)}) collective-permute-start(f32[32]{0:T(128)S(1)} %get-tuple-element.170), channel_id=1, source_target_pairs={{0,64},{1,65},{2,66},{3,67},{4,68},{5,69},{6,70},{7,71},{8,72},{9,... | collective-permute-start | bytes 392 | tf_op jit(solution)/shard_map/ppermute | solution.py:17
  711.6 46.2 %collective-permute-start.15 = (f32[32,64,64]{2,1,0:T(8,128)S(1)}, f32[32,64,64]{2,1,0:T(8,128)S(1)}, u32[]{:S(2)}, u32[]{:S(2)}) collective-permute-start(f32[32,64,64]{2,1,0:T(8,128)S(1)} %multiply_add_fusion.9), channel_id=1, source_target_pairs={{64,0},{65,1},{66,2},{67,3},{68,4},{69,5},{70,6},{71,7},{72,8},{73... | collective-permute-start | bytes 1572872 | tf_op jit(solution)/shard_map/ppermute | solution.py:17
  713.1 65.6 %collective-permute-start.32 = (f32[32,64,64]{2,1,0:T(8,128)S(1)}, f32[32,64,64]{2,1,0:T(8,128)S(1)}, u32[]{:S(2)}, u32[]{:S(2)}) collective-permute-start(f32[32,64,64]{2,1,0:T(8,128)S(1)} %multiply_add_fusion.1), channel_id=1, source_target_pairs={{0,64},{1,65},{2,66},{3,67},{4,68},{5,69},{6,70},{7,71},{8,72},{9,... | collective-permute-start | bytes 1572872 | tf_op jit(solution)/shard_map/ppermute | solution.py:17
  758.0 22.3 %collective-permute-start.16 = (f32[32,64,64]{2,1,0:T(8,128)S(1)}, f32[32,64,64]{2,1,0:T(8,128)S(1)}, u32[]{:S(2)}, u32[]{:S(2)}) collective-permute-start(f32[32,64,64]{2,1,0:T(8,128)S(1)} %multiply_add_fusion.8), channel_id=1, source_target_pairs={{128,0},{129,1},{130,2},{131,3},{132,4},{133,5},{134,6},{135,7},{1... | collective-permute-start | bytes 1572872 | tf_op jit(solution)/shard_map/ppermute | solution.py:17
  (21 other events, 898.8 us)
Sparse Core Ops, SparseCore 0:
  795.1 302.9 all-reduce.2
where the time goes:
time: 1110 us
  waiting for transfers between devices  446 us (40%)
  blocking collectives  348 us (31%)
  starting transfers between devices  268 us (24%)
  matrix products  19.8 us (2%)
  between operations  14.9 us (1%)
    all_gather x1, blocking collectives, per_device(): weights_full = lax.all_gather(w_bc, ('outer', 'inner'), axis=0, tiled=True)  348 us
    unnamed x2, waiting for transfers between devices  298 us
    ppermute x34, starting transfers between devices, shifted(): lax.ppermute(value, axis, [(source, source + steps) for source in range(f...  268 us
    ppermute x34, waiting for transfers between devices, shifted(): lax.ppermute(value, axis, [(source, source + steps) for source in range(f...  148 us
  transfers between devices with their start and end apart: 35, of which 11 were waited for; matrix products, arithmetic and copies ran while one was open for 2% of the time, Pallas kernels for 0%

commit v1 on v0

v1 whole, which is shorter than its diff:
```python
import functools
import math

import jax
import jax.numpy as jnp
from jax import lax
from jax.experimental import pallas as pl
from jax.experimental.pallas import tpu as pltpu
from jax.sharding import PartitionSpec as P

BF16 = jnp.bfloat16
F32 = jnp.float32
MESH = pl.DeviceIdType.MESH
HIGH = lax.Precision.HIGHEST

NN = (((1,), (0,)), ((), ()))
NT = (((1,), (1,)), ((), ()))

W_NEAR, W_FAR, S_OUT, S_FAR, S_BACK, S_HOME, G_FAR, G_NEAR = range(8)


def dot(a, b, dims=NN):
    return lax.dot_general(a, b, dims, preferred_element_type=F32)


def split(value):
    high = value.astype(BF16)
    return high, (value - high.astype(F32)).astype(BF16)


def dot3(a, b, dims=NN):
    a_high, a_low = split(a)
    b_high, b_low = split(b)
    return dot(a_high, b_high, dims) + dot(a_high, b_low, dims) + dot(a_low, b_high, dims)


def iota(shape, axis):
    return lax.broadcasted_iota(jnp.int32, shape, axis)


def kernel(
    scale, n_out, n_in,
    hidden_hbm, x_hbm, dt_ref, decay_ref, w_ref, gy_hbm,
    gx_hbm, gh_hbm, gp_ref,
    hidden, x, gy, hidden_t, gx, gh,
    w_near, w_far, grow, spread, xw_hi, xw_lo, gw_hi, gw_lo,
    s_send, s_recv, prefix, near_sum, o_send, o_recv, o_back, carry, s_back, s_home,
    g_send, g_recv, g_sum, g_near,
    load_sem, send_sem, recv_sem,
):
    me_out, me_in = lax.axis_index("outer"), lax.axis_index("inner")
    rows, width = hidden.shape
    lanes = x.shape[1]
    heads = dt_ref.shape[1]
    size = lanes // heads
    state = w_far.shape[2] // 2
    part = lanes // n_in
    far = 2 * state // n_out
    pairs = heads // 2

    loads = [
        pltpu.make_async_copy(source, target, load_sem.at[k])
        for k, (source, target) in enumerate(((x_hbm, x), (gy_hbm, gy), (hidden_hbm, hidden)))
    ]
    for load in loads:
        load.start()

    barrier = pltpu.get_barrier_semaphore()

    def each_near(act):
        lax.fori_loop(1, n_in, lambda k, c: (act(k, lax.rem(me_in + k, n_in)), c)[1], 0)

    def each_far(act):
        lax.fori_loop(1, n_out, lambda k, c: (act(k, lax.rem(me_out + k, n_out)), c)[1], 0)

    def greet(*place):
        pl.semaphore_signal(barrier, inc=1, device_id=place, device_id_type=MESH)

    each_near(lambda k, i: greet(me_out, i))
    each_far(lambda k, o: greet(o, me_in))

    def near_copy(phase, k, source, target, i):
        return pltpu.make_async_remote_copy(
            src_ref=source, dst_ref=target, send_sem=send_sem.at[phase, k], recv_sem=recv_sem.at[phase, k],
            device_id=(me_out, i), device_id_type=MESH,
        )

    def far_copy(phase, k, source, target, o):
        return pltpu.make_async_remote_copy(
            src_ref=source, dst_ref=target, send_sem=send_sem.at[phase, k], recv_sem=recv_sem.at[phase, k],
            device_id=(o, me_in), device_id_type=MESH,
        )

    own_rows = w_ref.shape[0]
    tile = w_near.shape[1]
    per_tile = tile // own_rows
    own_w = jnp.concatenate([w_ref[...].astype(F32)] * per_tile, axis=0)
    own_w = jnp.where(iota(own_w.shape, 0) // own_rows == lax.rem(me_in, per_tile), own_w, 0.0)
    w_near[me_in] = own_w

    pl.semaphore_wait(barrier, n_in + n_out - 2)
    each_near(lambda k, i: near_copy(W_NEAR, k, w_near.at[me_in], w_near.at[me_in], i).start())

    decay = decay_ref[...]
    causal = (iota((rows, rows), 0) >= iota((rows, rows), 1)).astype(F32)
    running = lax.dot_general(causal, decay, NN, precision=HIGH, preferred_element_type=F32)
    total = running[rows - 1:rows, :]
    dt = dt_ref[...]
    to_end = dt * jnp.exp(total - running)
    from_start = jnp.exp(running)
    shifted = running - jnp.log(dt)
    running_t = jnp.transpose(
        jnp.concatenate([running, jnp.zeros((rows, 128 - heads), F32)], axis=1)
    )

    each_near(lambda k, i: near_copy(W_NEAR, k, w_near.at[me_in], w_near.at[lax.rem(me_in + n_in - k, n_in)], i).wait_recv())
    block = [
        functools.reduce(lambda a, b: a + b, [w_near[t * per_tile + q] for q in range(per_tile)])
        for t in range(n_in // per_tile)
    ]
    w_far[me_out] = jnp.concatenate(block, axis=0).astype(BF16)
    each_far(lambda k, o: far_copy(W_FAR, k, w_far.at[me_out], w_far.at[me_out], o).start())

    stack = jnp.concatenate([to_end, from_start, jnp.broadcast_to(total, (8, heads))], axis=0)
    high = stack.astype(BF16)
    rest = stack - high.astype(F32)
    middle = rest.astype(BF16)
    low = (rest - middle.astype(F32)).astype(BF16)
    stack = jnp.concatenate([high, middle, low], axis=1)
    for load in loads:
        load.wait()
    for c in range(lanes // 256):
        at = slice(c * 256, (c + 1) * 256)
        chosen = lax.rem(iota((3 * heads, 256), 0), heads) == (iota((3 * heads, 256), 1) + c * 256) // size
        wide = dot(stack, jnp.where(chosen, 1.0, 0.0).astype(BF16))
        spread[:, at] = wide[:rows]
        xw_hi[:, at], xw_lo[:, at] = split(x[:, at].astype(F32) * wide[:rows])
        gw_hi[:, at], gw_lo[:, at] = split(gy[:, at].astype(F32) * wide[rows:2 * rows])
        for q in range(max(1, 256 // part)):
            lane = c * 256 + q * part
            cut = min(part, 256)
            s_send[lane // part, 2 * state:, lane % part:lane % part + cut] = wide[2 * rows:, q * part:q * part + cut]

    left = iota((rows, 2 * size), 1) < size
    keep = iota((rows, rows), 0) <= iota((rows, rows), 1)
    form = jnp.zeros((rows, rows), F32)

    def stacked(p):
        g = gy[:, p * 2 * size:(p + 1) * 2 * size]
        zero = jnp.zeros_like(g)
        return jnp.concatenate([jnp.where(left, g, zero), jnp.where(left, zero, g)], axis=0)

    for p in range(pairs):
        products = dot(x[:, p * 2 * size:(p + 1) * 2 * size], stacked(p), NT)
        for q in range(2):
            h = 2 * p + q
            spans = running_t[h:h + 1, :] - shifted[:, h:h + 1]
            factor = jnp.exp(jnp.where(keep, spans, -1e30))
            grow[h] = factor
            form = form + factor * products[:, q * rows:(q + 1) * rows]
    for c in range(width // 128):
        hidden_t[c * 128:(c + 1) * 128, :] = jnp.transpose(hidden[:, c * 128:(c + 1) * 128])

    each_far(lambda k, o: far_copy(W_FAR, k, w_far.at[me_out], w_far.at[lax.rem(me_out + n_out - k, n_out)], o).wait_recv())
    w = w_far[...].reshape(width, 2 * state)
    projected = dot(hidden[...], w)
    projected_t = jnp.transpose(projected)
    proj_hi, proj_lo = split(projected_t)
    b_t = jnp.concatenate([proj_hi[:state], proj_lo[:state]], axis=0)
    c_t = jnp.concatenate([proj_hi[state:], proj_lo[state:]], axis=0)

    def own_part(i):
        at = pl.ds(pl.multiple_of(i * part, part), part)
        forward = dot(b_t, xw_hi[:, at])
        s_send[i, :state, :] = forward[:state] + forward[state:] + dot(b_t[:state], xw_lo[:, at])
        backward = dot(c_t, gw_hi[:, at])
        s_send[i, state:2 * state, :] = backward[:state] + backward[state:] + dot(c_t[:state], gw_lo[:, at])

    def send_part(k, i):
        own_part(i)
        near_copy(S_OUT, k, s_send.at[i], s_recv.at[me_in], i).start()

    each_near(send_part)
    own_part(me_in)
    s_recv[me_in] = s_send[me_in]

    b_rows, c_rows = projected[:, :state], projected[:, state:]
    scores = dot3(b_rows, c_rows, NT)
    for p in range(pairs):
        mixed = jnp.concatenate([grow[2 * p] * scores, grow[2 * p + 1] * scores], axis=1).astype(BF16)
        gx[:, p * 2 * size:(p + 1) * 2 * size] = dot(mixed, stacked(p))
    near_b = dot3(form, c_rows)
    near_c = dot3(jnp.transpose(form), b_rows)

    each_near(lambda k, i: near_copy(S_OUT, k, s_send.at[i], s_recv.at[lax.rem(me_in + n_in - k, n_in)], i).wait_recv())

    totals = [s_recv[k, 2 * state:2 * state + 1, :] for k in range(n_in)]
    after, before = jnp.zeros((1, part), F32), jnp.zeros((1, part), F32)
    ahead, behind = [None] * n_in, [None] * n_in
    for k in range(n_in):
        ahead[k], behind[n_in - 1 - k] = jnp.exp(before), jnp.exp(after)
        before = before + totals[k]
        after = after + totals[n_in - 1 - k]
    steps = [jnp.exp(t) for t in totals]
    forward = jnp.zeros((state, part), F32)
    backward = jnp.zeros((state, part), F32)
    for k in range(n_in):
        prefix[k, :state, :] = forward
        forward = forward * steps[k] + s_recv[k, :state, :]
        b = n_in - 1 - k
        prefix[b, state:, :] = backward
        backward = backward * steps[b] + s_recv[b, state:2 * state, :]
    near_sum[:state] = forward
    near_sum[state:] = backward
    for o in range(n_out):
        o_send[o, :far, :] = near_sum[o * far:(o + 1) * far, :]
        o_send[o, far:, :] = jnp.broadcast_to(before, (8, part))
    each_far(lambda k, o: far_copy(S_FAR, k, o_send.at[o], o_recv.at[me_out], o).start())
    o_recv[me_out] = o_send[me_out]
    each_far(lambda k, o: far_copy(S_FAR, k, o_send.at[o], o_recv.at[lax.rem(me_out + n_out - k, n_out)], o).wait_recv())

    is_forward = me_out < n_out // 2
    held = jnp.zeros((far, part), F32)
    for k in range(n_out):
        at = jnp.where(is_forward, k, n_out - 1 - k)
        o_back[at] = held
        held = held * jnp.exp(o_recv[at, far:far + 1, :]) + o_recv[at, :far, :]
    each_far(lambda k, o: far_copy(S_BACK, k, o_back.at[o], carry.at[me_out], o).start())
    carry[me_out] = o_back[me_out]
    each_far(lambda k, o: far_copy(S_BACK, k, o_back.at[o], carry.at[lax.rem(me_out + n_out - k, n_out)], o).wait_recv())

    carried = carry[...].reshape(2 * state, part)
    for k in range(n_in):
        s_back[k, :state, :] = prefix[k, :state, :] + ahead[k] * carried[:state]
        s_back[k, state:, :] = prefix[k, state:, :] + behind[k] * carried[state:]
    each_near(lambda k, i: near_copy(S_HOME, k, s_back.at[i], s_home.at[me_in], i).start())
    s_home[me_in] = s_back[me_in]

    def use_part(i, sums):
        sum_b, sum_c = sums
        at = pl.ds(pl.multiple_of(i * part, part), part)
        got = s_home[i]
        got_hi, got_lo = split(got)
        for_c = jnp.concatenate([got_hi[:state], got_lo[:state]], axis=0)
        for_b = jnp.concatenate([got_hi[state:], got_lo[state:]], axis=0)
        wide_b, wide_c = dot(xw_hi[:, at], for_b, NT), dot(gw_hi[:, at], for_c, NT)
        sum_b = sum_b + wide_b[:, :state] + wide_b[:, state:] + dot(xw_lo[:, at], got_hi[state:], NT)
        sum_c = sum_c + wide_c[:, :state] + wide_c[:, state:] + dot(gw_lo[:, at], got_hi[:state], NT)
        return sum_b, sum_c

    def use_arrived(k, sums):
        i = lax.rem(me_in + n_in - k, n_in)
        near_copy(S_HOME, k, s_back.at[i], s_home.at[i], i).wait_recv()
        return use_part(i, sums)

    sums = use_part(me_in, (near_b, near_c))
    sums = lax.fori_loop(1, n_in, use_arrived, sums)
    d_low = jnp.concatenate(sums, axis=1).astype(BF16)

    cut = width // n_out
    for o in range(n_out):
        g_send[o] = (dot(hidden_t[o * cut:(o + 1) * cut, :], d_low) * scale).astype(BF16)
    each_far(lambda k, o: far_copy(G_FAR, k, g_send.at[o], g_recv.at[me_out], o).start())
    g_recv[me_out] = g_send[me_out]

    gh[...] = dot(d_low, w, NT)
    store_gh = pltpu.make_async_copy(gh, gh_hbm, load_sem.at[0])
    store_gh.start()

    each_far(lambda k, o: far_copy(G_FAR, k, g_send.at[o], g_recv.at[lax.rem(me_out + n_out - k, n_out)], o).wait_recv())
    g_sum[...] = functools.reduce(lambda a, b: a + b, [g_recv[o].astype(F32) for o in range(n_out)])

    def owned(i):
        return g_sum.at[pl.ds(pl.multiple_of(i // per_tile * tile, tile), tile), :]

    each_near(lambda k, i: near_copy(G_NEAR, k, owned(i), g_near.at[me_in], i).start())
    g_near[me_in] = g_sum[pl.ds(pl.multiple_of(me_in // per_tile * tile, tile), tile), :]

    b_hi, b_lo = split(b_rows)
    b_three = jnp.concatenate([b_hi, b_lo, b_hi], axis=1)
    for i in range(n_in):
        at = slice(i * part, (i + 1) * part)
        got_hi, got_lo = split(s_home[i, state:, :])
        gx[:, at] = gx[:, at] + spread[:, at] * dot(b_three, jnp.concatenate([got_hi, got_hi, got_lo], axis=0))
    store_gx = pltpu.make_async_copy(gx, gx_hbm, load_sem.at[1])
    store_gx.start()

    each_near(lambda k, i: near_copy(G_NEAR, k, owned(i), g_near.at[lax.rem(me_in + n_in - k, n_in)], i).wait_recv())
    summed = functools.reduce(lambda a, b: a + b, [g_near[i] for i in range(n_in)])
    mine = summed[:own_rows]
    for q in range(1, per_tile):
        mine = jnp.where(lax.rem(me_in, per_tile) == q, summed[q * own_rows:(q + 1) * own_rows], mine)
    gp_ref[...] = mine

    each_near(lambda k, i: near_copy(W_NEAR, k, w_near.at[me_in], w_near.at[me_in], i).wait_send())
    each_far(lambda k, o: far_copy(W_FAR, k, w_far.at[me_out], w_far.at[me_out], o).wait_send())
    each_near(lambda k, i: near_copy(S_OUT, k, s_send.at[i], s_recv.at[me_in], i).wait_send())
    each_far(lambda k, o: far_copy(S_FAR, k, o_send.at[o], o_recv.at[me_out], o).wait_send())
    each_far(lambda k, o: far_copy(S_BACK, k, o_back.at[o], carry.at[me_out], o).wait_send())
    each_near(lambda k, i: near_copy(S_HOME, k, s_back.at[i], s_home.at[me_in], i).wait_send())
    each_far(lambda k, o: far_copy(G_FAR, k, g_send.at[o], g_recv.at[me_out], o).wait_send())
    each_near(lambda k, i: near_copy(G_NEAR, k, owned(i), g_near.at[me_in], i).wait_send())
    store_gh.wait()
    store_gx.wait()


def per_device(hidden, x_act, dt_step, log_decay, w_bc, grad_y):
    n_out, n_in = lax.axis_size("outer"), lax.axis_size("inner")
    rows, width = hidden.shape
    lanes = x_act.shape[1]
    heads = dt_step.shape[1]
    own_rows, columns = w_bc.shape
    part = lanes // n_in
    far = columns // n_out
    tile = max(8, own_rows)
    most = max(n_out, n_in)
    scale = 1.0 / math.sqrt(rows * n_out * n_in)
    anywhere = pl.BlockSpec(memory_space=pl.ANY)
    vmem = pl.BlockSpec(memory_space=pltpu.VMEM)
    return pl.pallas_call(
        functools.partial(kernel, scale, n_out, n_in),
        out_shape=(
            jax.ShapeDtypeStruct((rows, lanes), F32),
            jax.ShapeDtypeStruct((rows, width), F32),
            jax.ShapeDtypeStruct((own_rows, columns), F32),
        ),
        in_specs=[anywhere, anywhere, vmem, vmem, vmem, anywhere],
        out_specs=(anywhere, anywhere, vmem),
        scratch_shapes=[
            pltpu.VMEM((rows, width), BF16),
            pltpu.VMEM((rows, lanes), BF16),
            pltpu.VMEM((rows, lanes), BF16),
            pltpu.VMEM((width, rows), BF16),
            pltpu.VMEM((rows, lanes), F32),
            pltpu.VMEM((rows, width), F32),
            pltpu.VMEM((n_in, tile, columns), F32),
            pltpu.VMEM((n_out, width // n_out, columns), BF16),
            pltpu.VMEM((heads, rows, rows), F32),
            pltpu.VMEM((rows, lanes), F32),
            pltpu.VMEM((rows, lanes), BF16),
            pltpu.VMEM((rows, lanes), BF16),
            pltpu.VMEM((rows, lanes), BF16),
            pltpu.VMEM((rows, lanes), BF16),
            pltpu.VMEM((n_in, columns + 8, part), F32),
            pltpu.VMEM((n_in, columns + 8, part), F32),
            pltpu.VMEM((n_in, columns, part), F32),
            pltpu.VMEM((columns, part), F32),
            pltpu.VMEM((n_out, far + 8, part), F32),
            pltpu.VMEM((n_out, far + 8, part), F32),
            pltpu.VMEM((n_out, far, part), F32),
            pltpu.VMEM((n_out, far, part), F32),
            pltpu.VMEM((n_in, columns, part), F32),
            pltpu.VMEM((n_in, columns, part), F32),
            pltpu.VMEM((n_out, width // n_out, columns), BF16),
            pltpu.VMEM((n_out, width // n_out, columns), BF16),
            pltpu.VMEM((width // n_out, columns), F32),
            pltpu.VMEM((n_in, tile, columns), F32),
            pltpu.SemaphoreType.DMA((3,)),
            pltpu.SemaphoreType.DMA((8, most)),
            pltpu.SemaphoreType.DMA((8, most)),
        ],
        compiler_params=pltpu.CompilerParams(
            collective_id=0, has_side_effects=True, vmem_limit_bytes=48 * 1024 * 1024
        ),
        cost_estimate=pl.CostEstimate(flops=10**9, bytes_accessed=3 * 10**6, transcendentals=10**6),
    )(hidden, x_act, dt_step, log_decay, w_bc, grad_y)


def solution(mesh):
    spec = P(("outer", "inner"), None)
    return jax.shard_map(
        per_device, mesh=mesh, in_specs=(spec,) * 6, out_specs=(spec,) * 3, check_vma=False
    )
```

time: 1110 us -> 91.9 us (0.08)
  waiting for transfers between devices: 446 us -> 0 us
  blocking collectives: 348 us -> 0 us
  starting transfers between devices: 268 us -> 0 us
  Pallas kernels: 0 us -> 84.1 us
  matrix products: 19.8 us -> 0 us
  between operations: 14.9 us -> 0.67 us
    all_gather x1 -> x0, blocking collectives: 348 us -> none  [per_device(): weights_full = lax.all_gather(w_bc, ('outer', 'inner'), axis=0, tiled=True)]
    unnamed x2 -> x0, waiting for transfers between devices: 298 us -> none
    ppermute x34 -> x0, starting transfers between devices: 268 us -> none  [shifted(): lax.ppermute(value, axis, [(source, source + steps) for source in range(f...]
    ppermute x34 -> x0, waiting for transfers between devices: 148 us -> none  [shifted(): lax.ppermute(value, axis, [(source, source + steps) for source in range(f...]
    pallas_call x0 -> x1, Pallas kernels: none -> 84.1 us  [per_device(): pl.pallas_call(functools.partial(kernel, scale, n_out, n_in), out_shape=(...]
    dot_general x13 -> x0, matrix products: 19.8 us -> none  [the longest x2 5.97 us: block_step(): jnp.einsum('hij,jhp->ihp', segment * scores[None], inputs, precision=HIGH)]
  transfers between devices with their start and end apart: 35 -> 0, of which waited for: 11 -> 0; matrix products, arithmetic and copies ran while one was open for 2% -> 0% of each run, Pallas kernels for 0% -> 0%
where the time goes in v1:
time: 91.9 us; the launch traced here: 91.6 us
  Pallas kernels  84.1 us (92%)
  local copies, waits for them, and re-layouts  6.87 us (7%)
    pallas_call x1, Pallas kernels, per_device(): pl.pallas_call(functools.partial(kernel, scale, n_out, n_in), out_shape=(...  84.1 us
    unnamed x15, local copies, waits for them, and re-layouts  6.87 us

profile of v1, /device:TPU:1, one launch (start us, length us, event | category | flops | bytes accessed | tf_op | source)
XLA Modules:
  0.0 91.6 jit_solution(16022368578562193336)
XLA Ops:
  0.6 0.0 copy-start.4
  0.6 0.8 copy.9.dt_ref
  1.5 0.0 copy-done.4
  1.5 0.0 copy-start.3
  1.5 0.1 copy.10.decay_ref
  1.6 0.6 copy-done.3
  2.2 0.0 copy-start
  2.2 1.0 %copy-done = bf16[128,2048]{1,0:T(8,128)(2,1)S(1)} copy-done((bf16[128,2048]{1,0:T(8,128)(2,1)S(1)}, bf16[128,2048]{1,0:T(8,128)(2,1)}, u32[]{:S(2)}) %copy-start) | copy-done | bytes 524312
  3.2 0.0 copy-start.1
  3.2 1.0 %copy-done.1 = bf16[128,2048]{1,0:T(8,128)(2,1)S(1)} copy-done((bf16[128,2048]{1,0:T(8,128)(2,1)S(1)}, bf16[128,2048]{1,0:T(8,128)(2,1)}, u32[]{:S(2)}) %copy-start.1) | copy-done | bytes 524312
  4.2 0.0 copy-start.2
  4.2 0.9 %copy-done.2 = bf16[128,1024]{1,0:T(8,128)(2,1)S(1)} copy-done((bf16[128,1024]{1,0:T(8,128)(2,1)S(1)}, bf16[128,1024]{1,0:T(8,128)(2,1)}, u32[]{:S(2)}) %copy-start.2) | copy-done | bytes 262168
  5.2 84.1 %shard_map.85 = (f32[128,2048]{1,0:T(8,128)S(1)}, f32[128,1024]{1,0:T(8,128)S(1)}, f32[4,128]{1,0:T(4,128)S(1)}) custom-call(bf16[128,1024]{1,0:T(8,128)(2,1)S(1)} %copy-done.2, bf16[128,2048]{1,0:T(8,128)(2,1)S(1)} %copy-done, f32[128,32]{1,0:T(8,128)S(1)} %copy.9.dt_ref, f32[128,32]{1,0:T(8,128)S(1)} %copy.10.decay_ref, bf16[4,128]{1,0:T(4,128)(2,1)S(1)} %copy-done.3, ...), custom_call_target="tpu_custom_call" | custom-call | flops 1000000000 | bytes 3000000 | tf_op jit(solution)/shard_map/pallas_call | solution.py:320
  89.3 1.0 %copy.14 = f32[128,2048]{1,0:T(8,128)} copy(f32[128,2048]{1,0:T(8,128)S(1)} %get-tuple-element.6) | data formatting | bytes 2097152
  90.3 0.8 copy.15
  91.1 0.6 copy.16
Async XLA Ops:
  0.6 0.8 copy-start.4
  1.5 0.7 copy-start.3
  2.2 1.0 %copy-start = (bf16[128,2048]{1,0:T(8,128)(2,1)S(1)}, bf16[128,2048]{1,0:T(8,128)(2,1)}, u32[]{:S(2)}) copy-start(bf16[128,2048]{1,0:T(8,128)(2,1)} %x_hbm.1) | copy-start | bytes 1572868
  3.2 1.0 %copy-start.1 = (bf16[128,2048]{1,0:T(8,128)(2,1)S(1)}, bf16[128,2048]{1,0:T(8,128)(2,1)}, u32[]{:S(2)}) copy-start(bf16[128,2048]{1,0:T(8,128)(2,1)} %gy_hbm.1) | copy-start | bytes 1572868
  4.2 0.9 %copy-start.2 = (bf16[128,1024]{1,0:T(8,128)(2,1)S(1)}, bf16[128,1024]{1,0:T(8,128)(2,1)}, u32[]{:S(2)}) copy-start(bf16[128,1024]{1,0:T(8,128)(2,1)} %hidden_hbm.1) | copy-start | bytes 786436

commit v2 on v1

--- a/solution.py
+++ b/solution.py
@@ -16,7 +16,10 @@
 NN = (((1,), (0,)), ((), ()))
 NT = (((1,), (1,)), ((), ()))
 
-W_NEAR, W_FAR, S_OUT, S_FAR, S_BACK, S_HOME, G_FAR, G_NEAR = range(8)
+W_NEAR, W_FAR, S_FAR, S_BACK, G_FAR, G_NEAR, S_OUT = range(7)
+PIECES = 2
+S_HOME = S_OUT + PIECES
+PHASES = S_HOME + PIECES
 
 
 def dot(a, b, dims=NN):
@@ -40,18 +43,18 @@
 
 def kernel(
     scale, n_out, n_in,
-    hidden_hbm, x_hbm, dt_ref, decay_ref, w_ref, gy_hbm,
+    hidden_hbm, x_hbm, dt_hbm, decay_hbm, w_ref, gy_hbm,
     gx_hbm, gh_hbm, gp_ref,
-    hidden, x, gy, hidden_t, gx, gh,
+    hidden, x, gy, dt_ref, decay_ref, hidden_t, gx, gh,
     w_near, w_far, grow, spread, xw_hi, xw_lo, gw_hi, gw_lo,
-    s_send, s_recv, prefix, near_sum, o_send, o_recv, o_back, carry, s_back, s_home,
+    s_send, s_recv, prefix, o_send, o_recv, o_back, carry, s_back, s_home,
     g_send, g_recv, g_sum, g_near,
     load_sem, send_sem, recv_sem,
 ):
     me_out, me_in = lax.axis_index("outer"), lax.axis_index("inner")
     rows, width = hidden.shape
     lanes = x.shape[1]
-    heads = dt_ref.shape[1]
+    heads = dt_ref.shape[0]
     size = lanes // heads
     state = w_far.shape[2] // 2
     part = lanes // n_in
@@ -60,7 +63,9 @@
 
     loads = [
         pltpu.make_async_copy(source, target, load_sem.at[k])
-        for k, (source, target) in enumerate(((x_hbm, x), (gy_hbm, gy), (hidden_hbm, hidden)))
+        for k, (source, target) in enumerate(
+            ((decay_hbm, decay_ref), (dt_hbm, dt_ref), (x_hbm, x), (gy_hbm, gy), (hidden_hbm, hidden))
+        )
     ]
     for load in loads:
         load.start()
@@ -101,33 +106,25 @@
     pl.semaphore_wait(barrier, n_in + n_out - 2)
     each_near(lambda k, i: near_copy(W_NEAR, k, w_near.at[me_in], w_near.at[me_in], i).start())
 
-    decay = decay_ref[...]
-    causal = (iota((rows, rows), 0) >= iota((rows, rows), 1)).astype(F32)
-    running = lax.dot_general(causal, decay, NN, precision=HIGH, preferred_element_type=F32)
-    total = running[rows - 1:rows, :]
-    dt = dt_ref[...]
-    to_end = dt * jnp.exp(total - running)
-    from_start = jnp.exp(running)
-    shifted = running - jnp.log(dt)
-    running_t = jnp.transpose(
-        jnp.concatenate([running, jnp.zeros((rows, 128 - heads), F32)], axis=1)
+    loads[0].wait()
+    loads[1].wait()
+    upto = (iota((rows, rows), 0) <= iota((rows, rows), 1)).astype(F32)
+    running_t = lax.dot_general(decay_ref[...], upto, NN, precision=HIGH, preferred_element_type=F32)
+    dt_t = dt_ref[...]
+    total_t = jnp.broadcast_to(running_t[:, rows - 1:], running_t.shape)
+    columns = jnp.transpose(jnp.concatenate(
+        [dt_t * jnp.exp(total_t - running_t), jnp.exp(running_t), total_t, running_t - jnp.log(dt_t)], axis=0
+    ))
+    shifted = columns[:, 3 * heads:]
+    stack = jnp.concatenate(
+        [columns[:, :heads], columns[:, heads:2 * heads], columns[:8, 2 * heads:3 * heads]], axis=0
     )
-
-    each_near(lambda k, i: near_copy(W_NEAR, k, w_near.at[me_in], w_near.at[lax.rem(me_in + n_in - k, n_in)], i).wait_recv())
-    block = [
-        functools.reduce(lambda a, b: a + b, [w_near[t * per_tile + q] for q in range(per_tile)])
-        for t in range(n_in // per_tile)
-    ]
-    w_far[me_out] = jnp.concatenate(block, axis=0).astype(BF16)
-    each_far(lambda k, o: far_copy(W_FAR, k, w_far.at[me_out], w_far.at[me_out], o).start())
-
-    stack = jnp.concatenate([to_end, from_start, jnp.broadcast_to(total, (8, heads))], axis=0)
     high = stack.astype(BF16)
     rest = stack - high.astype(F32)
     middle = rest.astype(BF16)
     low = (rest - middle.astype(F32)).astype(BF16)
     stack = jnp.concatenate([high, middle, low], axis=1)
-    for load in loads:
+    for load in loads[2:]:
         load.wait()
     for c in range(lanes // 256):
         at = slice(c * 256, (c + 1) * 256)
@@ -139,7 +136,15 @@
         for q in range(max(1, 256 // part)):
             lane = c * 256 + q * part
             cut = min(part, 256)
-            s_send[lane // part, 2 * state:, lane % part:lane % part + cut] = wide[2 * rows:, q * part:q * part + cut]
+            s_send[lane // part, :8, lane % part:lane % part + cut] = wide[2 * rows:, q * part:q * part + cut]
+
+    each_near(lambda k, i: near_copy(W_NEAR, k, w_near.at[me_in], w_near.at[lax.rem(me_in + n_in - k, n_in)], i).wait_recv())
+    block = [
+        functools.reduce(lambda a, b: a + b, [w_near[t * per_tile + q] for q in range(per_tile)])
+        for t in range(n_in // per_tile)
+    ]
+    w_far[me_out] = jnp.concatenate(block, axis=0).astype(BF16)
+    each_far(lambda k, o: far_copy(W_FAR, k, w_far.at[me_out], w_far.at[me_out], o).start())
 
     left = iota((rows, 2 * size), 1) < size
     keep = iota((rows, rows), 0) <= iota((rows, rows), 1)
@@ -169,19 +174,30 @@
     b_t = jnp.concatenate([proj_hi[:state], proj_lo[:state]], axis=0)
     c_t = jnp.concatenate([proj_hi[state:], proj_lo[state:]], axis=0)
 
-    def own_part(i):
+    step = 2 * state // PIECES
+
+    def rows_of(q):
+        return slice(8 + q * step if q else 0, 8 + (q + 1) * step)
+
+    def own_part(q, i):
         at = pl.ds(pl.multiple_of(i * part, part), part)
-        forward = dot(b_t, xw_hi[:, at])
-        s_send[i, :state, :] = forward[:state] + forward[state:] + dot(b_t[:state], xw_lo[:, at])
-        backward = dot(c_t, gw_hi[:, at])
-        s_send[i, state:2 * state, :] = backward[:state] + backward[state:] + dot(c_t[:state], gw_lo[:, at])
-
-    def send_part(k, i):
-        own_part(i)
-        near_copy(S_OUT, k, s_send.at[i], s_recv.at[me_in], i).start()
-
-    each_near(send_part)
-    own_part(me_in)
+        which = b_t if q == 0 else c_t
+        values, rests = (xw_hi, xw_lo) if q == 0 else (gw_hi, gw_lo)
+        both = dot(which, values[:, at])
+        s_send[i, 8 + q * state:8 + (q + 1) * state, :] = both[:state] + both[state:] + dot(which[:state], rests[:, at])
+
+    def out_copy(q, k, source, i):
+        return near_copy(S_OUT + q, k, s_send.at[i, rows_of(q)], s_recv.at[source, rows_of(q)], i)
+
+    half = PIECES // 2
+    for way in range(2):
+        def send_part(k, i, way=way):
+            own_part(way, i)
+            for q in range(way * half, (way + 1) * half):
+                out_copy(q, k, me_in, i).start()
+
+        each_near(send_part)
+        own_part(way, me_in)
     s_recv[me_in] = s_send[me_in]
 
     b_rows, c_rows = projected[:, :state], projected[:, state:]
@@ -192,69 +208,86 @@
     near_b = dot3(form, c_rows)
     near_c = dot3(jnp.transpose(form), b_rows)
 
-    each_near(lambda k, i: near_copy(S_OUT, k, s_send.at[i], s_recv.at[lax.rem(me_in + n_in - k, n_in)], i).wait_recv())
-
-    totals = [s_recv[k, 2 * state:2 * state + 1, :] for k in range(n_in)]
-    after, before = jnp.zeros((1, part), F32), jnp.zeros((1, part), F32)
-    ahead, behind = [None] * n_in, [None] * n_in
-    for k in range(n_in):
-        ahead[k], behind[n_in - 1 - k] = jnp.exp(before), jnp.exp(after)
-        before = before + totals[k]
-        after = after + totals[n_in - 1 - k]
-    steps = [jnp.exp(t) for t in totals]
-    forward = jnp.zeros((state, part), F32)
-    backward = jnp.zeros((state, part), F32)
-    for k in range(n_in):
-        prefix[k, :state, :] = forward
-        forward = forward * steps[k] + s_recv[k, :state, :]
-        b = n_in - 1 - k
-        prefix[b, state:, :] = backward
-        backward = backward * steps[b] + s_recv[b, state:2 * state, :]
-    near_sum[:state] = forward
-    near_sum[state:] = backward
-    for o in range(n_out):
-        o_send[o, :far, :] = near_sum[o * far:(o + 1) * far, :]
-        o_send[o, far:, :] = jnp.broadcast_to(before, (8, part))
-    each_far(lambda k, o: far_copy(S_FAR, k, o_send.at[o], o_recv.at[me_out], o).start())
-    o_recv[me_out] = o_send[me_out]
-    each_far(lambda k, o: far_copy(S_FAR, k, o_send.at[o], o_recv.at[lax.rem(me_out + n_out - k, n_out)], o).wait_recv())
-
-    is_forward = me_out < n_out // 2
-    held = jnp.zeros((far, part), F32)
-    for k in range(n_out):
-        at = jnp.where(is_forward, k, n_out - 1 - k)
-        o_back[at] = held
-        held = held * jnp.exp(o_recv[at, far:far + 1, :]) + o_recv[at, :far, :]
-    each_far(lambda k, o: far_copy(S_BACK, k, o_back.at[o], carry.at[me_out], o).start())
-    carry[me_out] = o_back[me_out]
-    each_far(lambda k, o: far_copy(S_BACK, k, o_back.at[o], carry.at[lax.rem(me_out + n_out - k, n_out)], o).wait_recv())
-
-    carried = carry[...].reshape(2 * state, part)
-    for k in range(n_in):
-        s_back[k, :state, :] = prefix[k, :state, :] + ahead[k] * carried[:state]
-        s_back[k, state:, :] = prefix[k, state:, :] + behind[k] * carried[state:]
-    each_near(lambda k, i: near_copy(S_HOME, k, s_back.at[i], s_home.at[me_in], i).start())
+    servers = n_out // PIECES
+
+    def far_send(q, k, o):
+        @pl.when(o // servers == q)
+        def _():
+            far_copy(S_FAR, k, o_send.at[o], o_recv.at[me_out], o).start()
+
+    def far_step(forward):
+        o_recv[me_out] = o_send[me_out]
+        each_far(lambda k, o: far_copy(S_FAR, k, o_send.at[o], o_recv.at[lax.rem(me_out + n_out - k, n_out)], o).wait_recv())
+        held = jnp.zeros((far, part), F32)
+        for k in range(n_out):
+            at = k if forward else n_out - 1 - k
+            o_back[at] = held
+            held = held * jnp.exp(o_recv[at, far:far + 1, :]) + o_recv[at, :far, :]
+        each_far(lambda k, o: far_copy(S_BACK, k, o_back.at[o], carry.at[me_out], o).start())
+        carry[me_out] = o_back[me_out]
+
+    for q in range(PIECES):
+        forward = q < half
+        each_near(lambda k, i: out_copy(q, k, lax.rem(me_in + n_in - k, n_in), i).wait_recv())
+        if q == 0:
+            totals = [s_recv[k, :1, :] for k in range(n_in)]
+            after, before = jnp.zeros((1, part), F32), jnp.zeros((1, part), F32)
+            ahead, behind = [None] * n_in, [None] * n_in
+            for k in range(n_in):
+                ahead[k], behind[n_in - 1 - k] = jnp.exp(before), jnp.exp(after)
+                before = before + totals[k]
+                after = after + totals[n_in - 1 - k]
+            steps = [jnp.exp(t) for t in totals]
+        held = jnp.zeros((step, part), F32)
+        for k in range(n_in) if forward else range(n_in - 1, -1, -1):
+            prefix[k, q * step:(q + 1) * step, :] = held
+            held = held * steps[k] + s_recv[k, 8 + q * step:8 + (q + 1) * step, :]
+        for j in range(servers):
+            o_send[q * servers + j, :far, :] = held[j * far:(j + 1) * far]
+            o_send[q * servers + j, far:, :] = jnp.broadcast_to(before, (8, part))
+        each_far(functools.partial(far_send, q))
+
+    for forward in (True, False):
+        pl.when((me_out < n_out // 2) == forward)(functools.partial(far_step, forward))
+
+    def back_wait(q, k, o):
+        source = lax.rem(me_out + n_out - k, n_out)
+
+        @pl.when(source // servers == q)
+        def _():
+            far_copy(S_BACK, k, o_back.at[o], carry.at[source], o).wait_recv()
+
+    def home_copy(q, k, source, i):
+        at = slice(q * step, (q + 1) * step)
+        return near_copy(S_HOME + q, k, s_back.at[i, at], s_home.at[source, at], i)
+
+    for q in range(PIECES):
+        each_far(functools.partial(back_wait, q))
+        carried = jnp.concatenate([carry[q * servers + j] for j in range(servers)], axis=0)
+        reach = ahead if q < half else behind
+        at = slice(q * step, (q + 1) * step)
+        for k in range(n_in):
+            s_back[k, at, :] = prefix[k, at, :] + reach[k] * carried
+        each_near(lambda k, i: home_copy(q, k, me_in, i).start())
     s_home[me_in] = s_back[me_in]
 
-    def use_part(i, sums):
-        sum_b, sum_c = sums
+    def use_part(way, i, sum_):
         at = pl.ds(pl.multiple_of(i * part, part), part)
-        got = s_home[i]
-        got_hi, got_lo = split(got)
-        for_c = jnp.concatenate([got_hi[:state], got_lo[:state]], axis=0)
-        for_b = jnp.concatenate([got_hi[state:], got_lo[state:]], axis=0)
-        wide_b, wide_c = dot(xw_hi[:, at], for_b, NT), dot(gw_hi[:, at], for_c, NT)
-        sum_b = sum_b + wide_b[:, :state] + wide_b[:, state:] + dot(xw_lo[:, at], got_hi[state:], NT)
-        sum_c = sum_c + wide_c[:, :state] + wide_c[:, state:] + dot(gw_lo[:, at], got_hi[:state], NT)
-        return sum_b, sum_c
-
-    def use_arrived(k, sums):
-        i = lax.rem(me_in + n_in - k, n_in)
-        near_copy(S_HOME, k, s_back.at[i], s_home.at[i], i).wait_recv()
-        return use_part(i, sums)
-
-    sums = use_part(me_in, (near_b, near_c))
-    sums = lax.fori_loop(1, n_in, use_arrived, sums)
+        values, rests = (gw_hi, gw_lo) if way == 0 else (xw_hi, xw_lo)
+        got_hi, got_lo = split(s_home[i, way * state:(way + 1) * state, :])
+        both = dot(values[:, at], jnp.concatenate([got_hi, got_lo], axis=0), NT)
+        return sum_ + both[:, :state] + both[:, state:] + dot(rests[:, at], got_hi, NT)
+
+    sums = []
+    for way, near in enumerate((near_c, near_b)):
+        def use_arrived(k, sum_, way=way):
+            i = lax.rem(me_in + n_in - k, n_in)
+            for q in range(way * half, (way + 1) * half):
+                home_copy(q, k, i, i).wait_recv()
+            return use_part(way, i, sum_)
+
+        sums.append(lax.fori_loop(1, n_in, use_arrived, use_part(way, me_in, near)))
+    sums = sums[::-1]
     d_low = jnp.concatenate(sums, axis=1).astype(BF16)
 
     cut = width // n_out
@@ -294,14 +327,33 @@
 
     each_near(lambda k, i: near_copy(W_NEAR, k, w_near.at[me_in], w_near.at[me_in], i).wait_send())
     each_far(lambda k, o: far_copy(W_FAR, k, w_far.at[me_out], w_far.at[me_out], o).wait_send())
-    each_near(lambda k, i: near_copy(S_OUT, k, s_send.at[i], s_recv.at[me_in], i).wait_send())
+    for q in range(PIECES):
+        each_near(lambda k, i: out_copy(q, k, me_in, i).wait_send())
+        each_near(lambda k, i: home_copy(q, k, me_in, i).wait_send())
     each_far(lambda k, o: far_copy(S_FAR, k, o_send.at[o], o_recv.at[me_out], o).wait_send())
     each_far(lambda k, o: far_copy(S_BACK, k, o_back.at[o], carry.at[me_out], o).wait_send())
-    each_near(lambda k, i: near_copy(S_HOME, k, s_back.at[i], s_home.at[me_in], i).wait_send())
     each_far(lambda k, o: far_copy(G_FAR, k, g_send.at[o], g_recv.at[me_out], o).wait_send())
     each_near(lambda k, i: near_copy(G_NEAR, k, owned(i), g_near.at[me_in], i).wait_send())
     store_gh.wait()
     store_gx.wait()
+
+
+def write_out(gx_from, gh_from, gp_from, gx_to, gh_to, gp_to, gx, gh, gp, sem):
+    pieces = gx.shape[1]
+    moves = [(gp_from, gp, gp_to)]
+    for q in range(gx.shape[0]):
+        at = slice(q * pieces, (q + 1) * pieces)
+        moves.append((gx_from.at[at], gx.at[q], gx_to.at[at]))
+        moves.append((gh_from.at[at], gh.at[q], gh_to.at[at]))
+    reads = [pltpu.make_async_copy(m[0], m[1], sem.at[0, k]) for k, m in enumerate(moves)]
+    writes = [pltpu.make_async_copy(m[1], m[2], sem.at[1, k]) for k, m in enumerate(moves)]
+    for read in reads:
+        read.start()
+    for read, write in zip(reads, writes):
+        read.wait()
+        write.start()
+    for write in writes:
+        write.wait()
 
 
 def per_device(hidden, x_act, dt_step, log_decay, w_bc, grad_y):
@@ -317,19 +369,21 @@
     scale = 1.0 / math.sqrt(rows * n_out * n_in)
     anywhere = pl.BlockSpec(memory_space=pl.ANY)
     vmem = pl.BlockSpec(memory_space=pltpu.VMEM)
-    return pl.pallas_call(
+    results = pl.pallas_call(
         functools.partial(kernel, scale, n_out, n_in),
         out_shape=(
             jax.ShapeDtypeStruct((rows, lanes), F32),
             jax.ShapeDtypeStruct((rows, width), F32),
             jax.ShapeDtypeStruct((own_rows, columns), F32),
         ),
-        in_specs=[anywhere, anywhere, vmem, vmem, vmem, anywhere],
+        in_specs=[anywhere, anywhere, anywhere, anywhere, vmem, anywhere],
         out_specs=(anywhere, anywhere, vmem),
         scratch_shapes=[
             pltpu.VMEM((rows, width), BF16),
             pltpu.VMEM((rows, lanes), BF16),
             pltpu.VMEM((rows, lanes), BF16),
+            pltpu.VMEM((heads, rows), F32),
+            pltpu.VMEM((heads, rows), F32),
             pltpu.VMEM((width, rows), BF16),
             pltpu.VMEM((rows, lanes), F32),
             pltpu.VMEM((rows, width), F32),
@@ -344,7 +398,6 @@
             pltpu.VMEM((n_in, columns + 8, part), F32),
             pltpu.VMEM((n_in, columns + 8, part), F32),
             pltpu.VMEM((n_in, columns, part), F32),
-            pltpu.VMEM((columns, part), F32),
             pltpu.VMEM((n_out, far + 8, part), F32),
             pltpu.VMEM((n_out, far + 8, part), F32),
             pltpu.VMEM((n_out, far, part), F32),
@@ -355,15 +408,29 @@
             pltpu.VMEM((n_out, width // n_out, columns), BF16),
             pltpu.VMEM((width // n_out, columns), F32),
             pltpu.VMEM((n_in, tile, columns), F32),
-            pltpu.SemaphoreType.DMA((3,)),
-            pltpu.SemaphoreType.DMA((8, most)),
-            pltpu.SemaphoreType.DMA((8, most)),
+            pltpu.SemaphoreType.DMA((5,)),
+            pltpu.SemaphoreType.DMA((PHASES, most)),
+            pltpu.SemaphoreType.DMA((PHASES, most)),
         ],
         compiler_params=pltpu.CompilerParams(
-            collective_id=0, has_side_effects=True, vmem_limit_bytes=48 * 1024 * 1024
+            collective_id=0, has_side_effects=True, vmem_limit_bytes=60 * 1024 * 1024
         ),
         cost_estimate=pl.CostEstimate(flops=10**9, bytes_accessed=3 * 10**6, transcendentals=10**6),
-    )(hidden, x_act, dt_step, log_decay, w_bc, grad_y)
+    )(hidden, x_act, dt_step.T, log_decay.T, w_bc, grad_y)
+    pieces = rows // 4
+    return pl.pallas_call(
+        write_out,
+        out_shape=tuple(jax.ShapeDtypeStruct(r.shape, r.dtype) for r in results),
+        in_specs=[anywhere] * 3,
+        out_specs=(anywhere,) * 3,
+        scratch_shapes=[
+            pltpu.VMEM((4, pieces, lanes), F32),
+            pltpu.VMEM((4, pieces, width), F32),
+            pltpu.VMEM((own_rows, columns), F32),
+            pltpu.SemaphoreType.DMA((2, 9)),
+        ],
+        compiler_params=pltpu.CompilerParams(vmem_limit_bytes=60 * 1024 * 1024),
+    )(*results)
 
 
 def solution(mesh):

time: 91.9 us -> 85 us (0.925)
  local copies, waits for them, and re-layouts: 6.87 us -> 0 us
    unnamed x15 -> x0, local copies, waits for them, and re-layouts: 6.87 us -> none
    pallas_call x0 -> x1, Pallas kernels: none -> 2.25 us  [per_device(): pl.pallas_call(write_out, out_shape=tuple((jax.ShapeDtypeStruct(r.shape,...]
    pallas_call x1, Pallas kernels: 84.1 us -> 82 us  [per_device(): pl.pallas_call(functools.partial(kernel, scale, n_out, n_in), out_shape=(...]
where the time goes in v2:
time: 85 us; the launch traced here: 84.9 us
  Pallas kernels  84.3 us (99%)
    pallas_call x1, Pallas kernels, per_device(): pl.pallas_call(functools.partial(kernel, scale, n_out, n_in), out_shape=(...  82 us
    pallas_call x1, Pallas kernels, per_device(): pl.pallas_call(write_out, out_shape=tuple((jax.ShapeDtypeStruct(r.shape,...  2.25 us

profile of v2, /device:TPU:1, one launch (start us, length us, event | category | flops | bytes accessed | tf_op | source)
XLA Modules:
  0.0 84.9 jit_solution(1145890651168016291)
XLA Ops:
  0.6 82.0 %shard_map.85 = (f32[128,2048]{1,0:T(8,128)}, f32[128,1024]{1,0:T(8,128)}, f32[4,128]{1,0:T(4,128)}) custom-call(bf16[128,1024]{1,0:T(8,128)(2,1)} %hidden_hbm.1, bf16[128,2048]{1,0:T(8,128)(2,1)} %x_hbm.1, f32[32,128]{1,0:T(8,128)} %bitcast.2, f32[32,128]{1,0:T(8,128)} %bitcast.3, bf16[4,128]{1,0:T(4,128)(2,1)} %w_ref.1, bf16[128,2048]{1,0:T(8,128)(2,1)} %gy_hbm.1), custom_call_target="tpu_custom_call" | custom-call | flops 1000000000 | bytes 3000000 | tf_op jit(solution)/shard_map/pallas_call | solution.py:372
  82.7 2.3 %shard_map.86 = (f32[128,2048]{1,0:T(8,128)}, f32[128,1024]{1,0:T(8,128)}, f32[4,128]{1,0:T(4,128)}) custom-call(f32[128,2048]{1,0:T(8,128)} %get-tuple-element.6.gx_from, f32[128,1024]{1,0:T(8,128)} %get-tuple-element.7.gh_from, f32[4,128]{1,0:T(4,128)} %get-tuple-element.8.gp_from), custom_call_target="tpu_custom_call" | custom-call | tf_op jit(solution)/shard_map/pallas_call | solution.py:421

commit v3 on v2

--- a/solution.py
+++ b/solution.py
@@ -17,9 +17,11 @@
 NT = (((1,), (1,)), ((), ()))
 
 W_NEAR, W_FAR, S_FAR, S_BACK, G_FAR, G_NEAR, S_OUT = range(7)
-PIECES = 2
-S_HOME = S_OUT + PIECES
-PHASES = S_HOME + PIECES
+WAYS = 2
+S_HOME = S_OUT + WAYS
+C_OUT = S_HOME + WAYS
+C_HOME = C_OUT + WAYS
+PHASES = C_HOME + WAYS
 
 
 def dot(a, b, dims=NN):
@@ -47,7 +49,7 @@
     gx_hbm, gh_hbm, gp_ref,
     hidden, x, gy, dt_ref, decay_ref, hidden_t, gx, gh,
     w_near, w_far, grow, spread, xw_hi, xw_lo, gw_hi, gw_lo,
-    s_send, s_recv, prefix, o_send, o_recv, o_back, carry, s_back, s_home,
+    c_send, c_recv, s_send, s_recv, prefix, o_send, o_recv, o_back, carry, s_back, s_home, c_back, states,
     g_send, g_recv, g_sum, g_near,
     load_sem, send_sem, recv_sem,
 ):
@@ -60,6 +62,9 @@
     part = lanes // n_in
     far = 2 * state // n_out
     pairs = heads // 2
+    n_chip = n_in // 2
+    chip, core = me_in // 2, lax.rem(me_in, 2)
+    other = 1 - core
 
     loads = [
         pltpu.make_async_copy(source, target, load_sem.at[k])
@@ -74,6 +79,9 @@
 
     def each_near(act):
         lax.fori_loop(1, n_in, lambda k, c: (act(k, lax.rem(me_in + k, n_in)), c)[1], 0)
+
+    def each_chip(act):
+        lax.fori_loop(1, n_chip, lambda k, c: (act(k, lax.rem(chip + k, n_chip)), c)[1], 0)
 
     def each_far(act):
         lax.fori_loop(1, n_out, lambda k, c: (act(k, lax.rem(me_out + k, n_out)), c)[1], 0)
@@ -136,7 +144,8 @@
         for q in range(max(1, 256 // part)):
             lane = c * 256 + q * part
             cut = min(part, 256)
-            s_send[lane // part, :8, lane % part:lane % part + cut] = wide[2 * rows:, q * part:q * part + cut]
+            i = lane // part
+            c_send[i % 2, i // 2, :8, lane % part:lane % part + cut] = wide[2 * rows:, q * part:q * part + cut]
 
     each_near(lambda k, i: near_copy(W_NEAR, k, w_near.at[me_in], w_near.at[lax.rem(me_in + n_in - k, n_in)], i).wait_recv())
     block = [
@@ -174,31 +183,71 @@
     b_t = jnp.concatenate([proj_hi[:state], proj_lo[:state]], axis=0)
     c_t = jnp.concatenate([proj_hi[state:], proj_lo[state:]], axis=0)
 
-    step = 2 * state // PIECES
-
-    def rows_of(q):
-        return slice(8 + q * step if q else 0, 8 + (q + 1) * step)
-
-    def own_part(q, i):
-        at = pl.ds(pl.multiple_of(i * part, part), part)
-        which = b_t if q == 0 else c_t
-        values, rests = (xw_hi, xw_lo) if q == 0 else (gw_hi, gw_lo)
+    def rows_of(way):
+        return slice(8 + state, 8 + 2 * state) if way else slice(0, 8 + state)
+
+    def state_rows(way, first=8):
+        return slice(first + way * state, first + (way + 1) * state)
+
+    def lanes_of(side, t):
+        return pl.ds(pl.multiple_of((t * 2 + side) * part, part), part)
+
+    def own_part(way, side, t):
+        at = lanes_of(side, t)
+        which = c_t if way else b_t
+        values, rests = (gw_hi, gw_lo) if way else (xw_hi, xw_lo)
         both = dot(which, values[:, at])
-        s_send[i, 8 + q * state:8 + (q + 1) * state, :] = both[:state] + both[state:] + dot(which[:state], rests[:, at])
-
-    def out_copy(q, k, source, i):
-        return near_copy(S_OUT + q, k, s_send.at[i, rows_of(q)], s_recv.at[source, rows_of(q)], i)
-
-    half = PIECES // 2
-    for way in range(2):
-        def send_part(k, i, way=way):
-            own_part(way, i)
-            for q in range(way * half, (way + 1) * half):
-                out_copy(q, k, me_in, i).start()
-
-        each_near(send_part)
-        own_part(way, me_in)
-    s_recv[me_in] = s_send[me_in]
+        c_send[side, t, state_rows(way), :] = both[:state] + both[state:] + dot(which[:state], rests[:, at])
+
+    def core_out(way, k, t):
+        return near_copy(C_OUT + way, k, c_send.at[other, t, rows_of(way)], c_recv.at[t, rows_of(way)], chip * 2 + other)
+
+    def chip_out(way, k, t, source):
+        return near_copy(S_OUT + way, k, s_send.at[t, rows_of(way)], s_recv.at[source, rows_of(way)], t * 2 + core)
+
+    def each_slice(act):
+        lax.fori_loop(1, n_chip + 1, lambda k, c: (act(k, lax.rem(chip + k, n_chip)), c)[1], 0)
+
+    def give(way):
+        def one(k, t):
+            own_part(way, other, t)
+            core_out(way, k, t).start()
+
+        each_slice(one)
+
+    first_core = core == 0
+
+    def join(way):
+        def one(k, t):
+            core_out(way, k, t).wait_recv()
+            own_total, other_total = c_send[core, t, :1, :], c_recv[t, :1, :]
+            ones = jnp.ones_like(own_total)
+            own_factor, other_factor = jnp.exp(other_total), jnp.exp(own_total)
+            own_is_far = first_core if way == 0 else jnp.logical_not(first_core)
+            at = state_rows(way)
+            s_send[t, at, :] = (
+                jnp.where(own_is_far, own_factor, ones) * c_send[core, t, at, :]
+                + jnp.where(own_is_far, ones, other_factor) * c_recv[t, at, :]
+            )
+            if way == 0:
+                s_send[t, :8, :] = c_send[core, t, :8, :] + c_recv[t, :8, :]
+
+            @pl.when(k < n_chip)
+            def _():
+                chip_out(way, k, t, chip).start()
+
+            @pl.when(k == n_chip)
+            def _():
+                s_recv[t, rows_of(way)] = s_send[t, rows_of(way)]
+
+        each_slice(one)
+
+    give(0)
+    each_slice(lambda k, t: own_part(0, core, t))
+    give(1)
+    join(0)
+    each_slice(lambda k, t: own_part(1, core, t))
+    join(1)
 
     b_rows, c_rows = projected[:, :state], projected[:, state:]
     scores = dot3(b_rows, c_rows, NT)
@@ -208,7 +257,7 @@
     near_b = dot3(form, c_rows)
     near_c = dot3(jnp.transpose(form), b_rows)
 
-    servers = n_out // PIECES
+    servers = n_out // 2
 
     def far_send(q, k, o):
         @pl.when(o // servers == q)
@@ -226,27 +275,25 @@
         each_far(lambda k, o: far_copy(S_BACK, k, o_back.at[o], carry.at[me_out], o).start())
         carry[me_out] = o_back[me_out]
 
-    for q in range(PIECES):
-        forward = q < half
-        each_near(lambda k, i: out_copy(q, k, lax.rem(me_in + n_in - k, n_in), i).wait_recv())
-        if q == 0:
-            totals = [s_recv[k, :1, :] for k in range(n_in)]
+    for way in range(WAYS):
+        each_chip(lambda k, t: chip_out(way, k, t, lax.rem(chip + n_chip - k, n_chip)).wait_recv())
+        if way == 0:
+            totals = [s_recv[k, :1, :] for k in range(n_chip)]
             after, before = jnp.zeros((1, part), F32), jnp.zeros((1, part), F32)
-            ahead, behind = [None] * n_in, [None] * n_in
-            for k in range(n_in):
-                ahead[k], behind[n_in - 1 - k] = jnp.exp(before), jnp.exp(after)
+            ahead, behind = [None] * n_chip, [None] * n_chip
+            for k in range(n_chip):
+                ahead[k], behind[n_chip - 1 - k] = jnp.exp(before), jnp.exp(after)
                 before = before + totals[k]
-                after = after + totals[n_in - 1 - k]
+                after = after + totals[n_chip - 1 - k]
             steps = [jnp.exp(t) for t in totals]
-        held = jnp.zeros((step, part), F32)
-        for k in range(n_in) if forward else range(n_in - 1, -1, -1):
-            prefix[k, q * step:(q + 1) * step, :] = held
-            held = held * steps[k] + s_recv[k, 8 + q * step:8 + (q + 1) * step, :]
+        held = jnp.zeros((state, part), F32)
+        for k in range(n_chip - 1, -1, -1) if way else range(n_chip):
+            prefix[k, state_rows(way, 0), :] = held
+            held = held * steps[k] + s_recv[k, state_rows(way), :]
         for j in range(servers):
-            o_send[q * servers + j, :far, :] = held[j * far:(j + 1) * far]
-            o_send[q * servers + j, far:, :] = jnp.broadcast_to(before, (8, part))
-        each_far(functools.partial(far_send, q))
-
+            o_send[way * servers + j, :far, :] = held[j * far:(j + 1) * far]
+            o_send[way * servers + j, far:, :] = jnp.broadcast_to(before, (8, part))
+        each_far(functools.partial(far_send, way))
     for forward in (True, False):
         pl.when((me_out < n_out // 2) == forward)(functools.partial(far_step, forward))
 
@@ -257,36 +304,62 @@
         def _():
             far_copy(S_BACK, k, o_back.at[o], carry.at[source], o).wait_recv()
 
-    def home_copy(q, k, source, i):
-        at = slice(q * step, (q + 1) * step)
-        return near_copy(S_HOME + q, k, s_back.at[i, at], s_home.at[source, at], i)
-
-    for q in range(PIECES):
-        each_far(functools.partial(back_wait, q))
-        carried = jnp.concatenate([carry[q * servers + j] for j in range(servers)], axis=0)
-        reach = ahead if q < half else behind
-        at = slice(q * step, (q + 1) * step)
-        for k in range(n_in):
+    def home_copy(way, k, t, source):
+        at = state_rows(way, 0)
+        return near_copy(S_HOME + way, k, s_back.at[t, at], s_home.at[source, at], t * 2 + core)
+
+    for way in range(WAYS):
+        each_far(functools.partial(back_wait, way))
+        carried = jnp.concatenate([carry[way * servers + j] for j in range(servers)], axis=0)
+        reach = behind if way else ahead
+        at = state_rows(way, 0)
+        for k in range(n_chip):
             s_back[k, at, :] = prefix[k, at, :] + reach[k] * carried
-        each_near(lambda k, i: home_copy(q, k, me_in, i).start())
-    s_home[me_in] = s_back[me_in]
-
-    def use_part(way, i, sum_):
-        at = pl.ds(pl.multiple_of(i * part, part), part)
-        values, rests = (gw_hi, gw_lo) if way == 0 else (xw_hi, xw_lo)
-        got_hi, got_lo = split(s_home[i, way * state:(way + 1) * state, :])
+        each_chip(lambda k, t: home_copy(way, k, t, chip).start())
+        s_home[chip, at, :] = s_back[chip, at, :]
+
+    def core_home(way, k, side, t):
+        at = state_rows(way, 0)
+        return near_copy(C_HOME + way, k, c_back.at[t, at], states.at[side, t, at], chip * 2 + other)
+
+    def use_part(way, side, t, sum_):
+        at = lanes_of(side, t)
+        values, rests = (xw_hi, xw_lo) if way else (gw_hi, gw_lo)
+        got_hi, got_lo = split(states[side, t, state_rows(way, 0), :])
         both = dot(values[:, at], jnp.concatenate([got_hi, got_lo], axis=0), NT)
         return sum_ + both[:, :state] + both[:, state:] + dot(rests[:, at], got_hi, NT)
 
+    def source_of(k):
+        return lax.rem(chip + n_chip - k, n_chip)
+
+    def share(way, k):
+        t = source_of(k)
+        at, tall = state_rows(way, 0), state_rows(way)
+        got = s_home[t, at, :]
+        by_own = jnp.exp(c_send[core, t, :1, :]) * got + c_send[core, t, tall, :]
+        by_other = jnp.exp(c_recv[t, :1, :]) * got + c_recv[t, tall, :]
+        comes_first = first_core if way == 0 else jnp.logical_not(first_core)
+        states[core, t, at, :] = jnp.where(comes_first, got, by_other)
+        c_back[t, at, :] = jnp.where(comes_first, by_own, got)
+        core_home(way, k, core, t).start()
+
     sums = []
     for way, near in enumerate((near_c, near_b)):
-        def use_arrived(k, sum_, way=way):
-            i = lax.rem(me_in + n_in - k, n_in)
-            for q in range(way * half, (way + 1) * half):
-                home_copy(q, k, i, i).wait_recv()
-            return use_part(way, i, sum_)
-
-        sums.append(lax.fori_loop(1, n_in, use_arrived, use_part(way, me_in, near)))
+        def share_arrived(k, sum_, way=way):
+            t = source_of(k)
+            home_copy(way, k, t, t).wait_recv()
+            share(way, k)
+            return use_part(way, core, t, sum_)
+
+        def use_other(k, sum_, way=way):
+            t = source_of(k)
+            core_home(way, k, other, t).wait_recv()
+            return use_part(way, other, t, sum_)
+
+        share(way, 0)
+        sum_ = use_part(way, core, chip, near)
+        sum_ = lax.fori_loop(1, n_chip, share_arrived, sum_)
+        sums.append(lax.fori_loop(0, n_chip, use_other, sum_))
     sums = sums[::-1]
     d_low = jnp.concatenate(sums, axis=1).astype(BF16)
 
@@ -313,7 +386,7 @@
     b_three = jnp.concatenate([b_hi, b_lo, b_hi], axis=1)
     for i in range(n_in):
         at = slice(i * part, (i + 1) * part)
-        got_hi, got_lo = split(s_home[i, state:, :])
+        got_hi, got_lo = split(states[i % 2, i // 2, state:, :])
         gx[:, at] = gx[:, at] + spread[:, at] * dot(b_three, jnp.concatenate([got_hi, got_hi, got_lo], axis=0))
     store_gx = pltpu.make_async_copy(gx, gx_hbm, load_sem.at[1])
     store_gx.start()
@@ -327,9 +400,11 @@
 
     each_near(lambda k, i: near_copy(W_NEAR, k, w_near.at[me_in], w_near.at[me_in], i).wait_send())
     each_far(lambda k, o: far_copy(W_FAR, k, w_far.at[me_out], w_far.at[me_out], o).wait_send())
-    for q in range(PIECES):
-        each_near(lambda k, i: out_copy(q, k, me_in, i).wait_send())
-        each_near(lambda k, i: home_copy(q, k, me_in, i).wait_send())
+    for way in range(WAYS):
+        each_slice(lambda k, t: core_out(way, k, t).wait_send())
+        each_chip(lambda k, t: chip_out(way, k, t, chip).wait_send())
+        each_chip(lambda k, t: home_copy(way, k, t, chip).wait_send())
+        each_slice(lambda k, t: core_home(way, k - 1, core, source_of(k - 1)).wait_send())
     each_far(lambda k, o: far_copy(S_FAR, k, o_send.at[o], o_recv.at[me_out], o).wait_send())
     each_far(lambda k, o: far_copy(S_BACK, k, o_back.at[o], carry.at[me_out], o).wait_send())
     each_far(lambda k, o: far_copy(G_FAR, k, g_send.at[o], g_recv.at[me_out], o).wait_send())
@@ -395,15 +470,19 @@
             pltpu.VMEM((rows, lanes), BF16),
             pltpu.VMEM((rows, lanes), BF16),
             pltpu.VMEM((rows, lanes), BF16),
-            pltpu.VMEM((n_in, columns + 8, part), F32),
-            pltpu.VMEM((n_in, columns + 8, part), F32),
-            pltpu.VMEM((n_in, columns, part), F32),
+            pltpu.VMEM((2, n_in // 2, columns + 8, part), F32),
+            pltpu.VMEM((n_in // 2, columns + 8, part), F32),
+            pltpu.VMEM((n_in // 2, columns + 8, part), F32),
+            pltpu.VMEM((n_in // 2, columns + 8, part), F32),
+            pltpu.VMEM((n_in // 2, columns, part), F32),
             pltpu.VMEM((n_out, far + 8, part), F32),
             pltpu.VMEM((n_out, far + 8, part), F32),
             pltpu.VMEM((n_out, far, part), F32),
             pltpu.VMEM((n_out, far, part), F32),
-            pltpu.VMEM((n_in, columns, part), F32),
-            pltpu.VMEM((n_in, columns, part), F32),
+            pltpu.VMEM((n_in // 2, columns, part), F32),
+            pltpu.VMEM((n_in // 2, columns, part), F32),
+            pltpu.VMEM((n_in // 2, columns, part), F32),
+            pltpu.VMEM((2, n_in // 2, columns, part), F32),
             pltpu.VMEM((n_out, width // n_out, columns), BF16),
             pltpu.VMEM((n_out, width // n_out, columns), BF16),
             pltpu.VMEM((width // n_out, columns), F32),

time: 85 us -> 82.8 us (0.974)
  Pallas kernels: 84.3 us -> 82 us
    pallas_call x1, Pallas kernels: 82 us -> 79.8 us  [per_device(): pl.pallas_call(functools.partial(kernel, scale, n_out, n_in), out_shape=(...]
where the time goes in v3:
time: 82.8 us; the launch traced here: 82.7 us
  Pallas kernels  82 us (99%)
    pallas_call x1, Pallas kernels, per_device(): pl.pallas_call(functools.partial(kernel, scale, n_out, n_in), out_shape=(...  79.8 us
    pallas_call x1, Pallas kernels, per_device(): pl.pallas_call(write_out, out_shape=tuple((jax.ShapeDtypeStruct(r.shape,...  2.25 us

profile of v3, /device:TPU:1, one launch (start us, length us, event | category | flops | bytes accessed | tf_op | source)
XLA Modules:
  0.0 82.7 jit_solution(3673683603897905723)
XLA Ops:
  0.6 79.8 %shard_map.85 = (f32[128,2048]{1,0:T(8,128)}, f32[128,1024]{1,0:T(8,128)}, f32[4,128]{1,0:T(4,128)}) custom-call(bf16[128,1024]{1,0:T(8,128)(2,1)} %hidden_hbm.1, bf16[128,2048]{1,0:T(8,128)(2,1)} %x_hbm.1, f32[32,128]{1,0:T(8,128)} %bitcast.2, f32[32,128]{1,0:T(8,128)} %bitcast.3, bf16[4,128]{1,0:T(4,128)(2,1)} %w_ref.1, bf16[128,2048]{1,0:T(8,128)(2,1)} %gy_hbm.1), custom_call_target="tpu_custom_call" | custom-call | flops 1000000000 | bytes 3000000 | tf_op jit(solution)/shard_map/pallas_call | solution.py:447
  80.4 2.3 %shard_map.86 = (f32[128,2048]{1,0:T(8,128)}, f32[128,1024]{1,0:T(8,128)}, f32[4,128]{1,0:T(4,128)}) custom-call(f32[128,2048]{1,0:T(8,128)} %get-tuple-element.6.gx_from, f32[128,1024]{1,0:T(8,128)} %get-tuple-element.7.gh_from, f32[4,128]{1,0:T(4,128)} %get-tuple-element.8.gp_from), custom_call_target="tpu_custom_call" | custom-call | tf_op jit(solution)/shard_map/pallas_call | solution.py:500

commit v4 on v3

--- a/solution.py
+++ b/solution.py
@@ -192,12 +192,16 @@
     def lanes_of(side, t):
         return pl.ds(pl.multiple_of((t * 2 + side) * part, part), part)
 
-    def own_part(way, side, t):
-        at = lanes_of(side, t)
+    def side_lanes(ref, side):
+        return jnp.concatenate([ref[:, lanes_of(side, t)] for t in range(n_chip)], axis=1)
+
+    def own_half(way, side):
         which = c_t if way else b_t
         values, rests = (gw_hi, gw_lo) if way else (xw_hi, xw_lo)
-        both = dot(which, values[:, at])
-        c_send[side, t, state_rows(way), :] = both[:state] + both[state:] + dot(which[:state], rests[:, at])
+        both = dot(which, side_lanes(values, side))
+        made = both[:state] + both[state:] + dot(which[:state], side_lanes(rests, side))
+        for t in range(n_chip):
+            c_send[side, t, state_rows(way), :] = made[:, t * part:(t + 1) * part]
 
     def core_out(way, k, t):
         return near_copy(C_OUT + way, k, c_send.at[other, t, rows_of(way)], c_recv.at[t, rows_of(way)], chip * 2 + other)
@@ -209,11 +213,8 @@
         lax.fori_loop(1, n_chip + 1, lambda k, c: (act(k, lax.rem(chip + k, n_chip)), c)[1], 0)
 
     def give(way):
-        def one(k, t):
-            own_part(way, other, t)
-            core_out(way, k, t).start()
-
-        each_slice(one)
+        own_half(way, other)
+        each_slice(lambda k, t: core_out(way, k, t).start())
 
     first_core = core == 0
 
@@ -243,10 +244,10 @@
         each_slice(one)
 
     give(0)
-    each_slice(lambda k, t: own_part(0, core, t))
+    own_half(0, core)
     give(1)
     join(0)
-    each_slice(lambda k, t: own_part(1, core, t))
+    own_half(1, core)
     join(1)
 
     b_rows, c_rows = projected[:, :state], projected[:, state:]
@@ -322,12 +323,12 @@
         at = state_rows(way, 0)
         return near_copy(C_HOME + way, k, c_back.at[t, at], states.at[side, t, at], chip * 2 + other)
 
-    def use_part(way, side, t, sum_):
-        at = lanes_of(side, t)
+    def use_half(way, side, sum_):
         values, rests = (xw_hi, xw_lo) if way else (gw_hi, gw_lo)
-        got_hi, got_lo = split(states[side, t, state_rows(way, 0), :])
-        both = dot(values[:, at], jnp.concatenate([got_hi, got_lo], axis=0), NT)
-        return sum_ + both[:, :state] + both[:, state:] + dot(rests[:, at], got_hi, NT)
+        got = jnp.concatenate([states[side, t, state_rows(way, 0), :] for t in range(n_chip)], axis=1)
+        got_hi, got_lo = split(got)
+        both = dot(side_lanes(values, side), jnp.concatenate([got_hi, got_lo], axis=0), NT)
+        return sum_ + both[:, :state] + both[:, state:] + dot(side_lanes(rests, side), got_hi, NT)
 
     def source_of(k):
         return lax.rem(chip + n_chip - k, n_chip)
@@ -345,27 +346,24 @@
 
     sums = []
     for way, near in enumerate((near_c, near_b)):
-        def share_arrived(k, sum_, way=way):
-            t = source_of(k)
-            home_copy(way, k, t, t).wait_recv()
+        def share_arrived(k, t):
+            source = source_of(k)
+            home_copy(way, k, source, source).wait_recv()
             share(way, k)
-            return use_part(way, core, t, sum_)
-
-        def use_other(k, sum_, way=way):
-            t = source_of(k)
-            core_home(way, k, other, t).wait_recv()
-            return use_part(way, other, t, sum_)
 
         share(way, 0)
-        sum_ = use_part(way, core, chip, near)
-        sum_ = lax.fori_loop(1, n_chip, share_arrived, sum_)
-        sums.append(lax.fori_loop(0, n_chip, use_other, sum_))
+        each_chip(share_arrived)
+        sum_ = use_half(way, core, near)
+        each_slice(lambda k, t: core_home(way, k - 1, other, source_of(k - 1)).wait_recv())
+        sums.append(use_half(way, other, sum_))
     sums = sums[::-1]
     d_low = jnp.concatenate(sums, axis=1).astype(BF16)
 
     cut = width // n_out
-    for o in range(n_out):
-        g_send[o] = (dot(hidden_t[o * cut:(o + 1) * cut, :], d_low) * scale).astype(BF16)
+    for q in range(2):
+        term = (dot(hidden_t[q * width // 2:(q + 1) * width // 2, :], d_low) * scale).astype(BF16)
+        for o in range(n_out // 2):
+            g_send[q * n_out // 2 + o] = term[o * cut:(o + 1) * cut]
     each_far(lambda k, o: far_copy(G_FAR, k, g_send.at[o], g_recv.at[me_out], o).start())
     g_recv[me_out] = g_send[me_out]
 

time: 82.8 us -> 77.8 us (0.940)
  Pallas kernels: 82 us -> 77 us
    pallas_call x1, Pallas kernels: 79.8 us -> 74.8 us  [per_device(): pl.pallas_call(functools.partial(kernel, scale, n_out, n_in), out_shape=(...]
where the time goes in v4:
time: 77.8 us; the launch traced here: 77.7 us
  Pallas kernels  77 us (99%)
    pallas_call x1, Pallas kernels, per_device(): pl.pallas_call(functools.partial(kernel, scale, n_out, n_in), out_shape=(...  74.8 us
    pallas_call x1, Pallas kernels, per_device(): pl.pallas_call(write_out, out_shape=tuple((jax.ShapeDtypeStruct(r.shape,...  2.25 us

profile of v4, /device:TPU:1, one launch (start us, length us, event | category | flops | bytes accessed | tf_op | source)
XLA Modules:
  0.0 77.7 jit_solution(7623477026766012837)
XLA Ops:
  0.6 74.8 %shard_map.85 = (f32[128,2048]{1,0:T(8,128)}, f32[128,1024]{1,0:T(8,128)}, f32[4,128]{1,0:T(4,128)}) custom-call(bf16[128,1024]{1,0:T(8,128)(2,1)} %hidden_hbm.1, bf16[128,2048]{1,0:T(8,128)(2,1)} %x_hbm.1, f32[32,128]{1,0:T(8,128)} %bitcast.2, f32[32,128]{1,0:T(8,128)} %bitcast.3, bf16[4,128]{1,0:T(4,128)(2,1)} %w_ref.1, bf16[128,2048]{1,0:T(8,128)(2,1)} %gy_hbm.1), custom_call_target="tpu_custom_call" | custom-call | flops 1000000000 | bytes 3000000 | tf_op jit(solution)/shard_map/pallas_call | solution.py:445
  75.4 2.3 %shard_map.86 = (f32[128,2048]{1,0:T(8,128)}, f32[128,1024]{1,0:T(8,128)}, f32[4,128]{1,0:T(4,128)}) custom-call(f32[128,2048]{1,0:T(8,128)} %get-tuple-element.6.gx_from, f32[128,1024]{1,0:T(8,128)} %get-tuple-element.7.gh_from, f32[4,128]{1,0:T(4,128)} %get-tuple-element.8.gp_from), custom_call_target="tpu_custom_call" | custom-call | tf_op jit(solution)/shard_map/pallas_call | solution.py:498

commit v5 on v4

--- a/solution.py
+++ b/solution.py
@@ -16,12 +16,13 @@
 NN = (((1,), (0,)), ((), ()))
 NT = (((1,), (1,)), ((), ()))
 
-W_NEAR, W_FAR, S_FAR, S_BACK, G_FAR, G_NEAR, S_OUT = range(7)
+W_NEAR, W_FAR, S_FAR, S_BACK, G_NEAR, S_OUT = range(6)
 WAYS = 2
 S_HOME = S_OUT + WAYS
 C_OUT = S_HOME + WAYS
 C_HOME = C_OUT + WAYS
-PHASES = C_HOME + WAYS
+G_FAR = C_HOME + WAYS
+PHASES = G_FAR + WAYS
 
 
 def dot(a, b, dims=NN):
@@ -172,8 +173,15 @@
             factor = jnp.exp(jnp.where(keep, spans, -1e30))
             grow[h] = factor
             form = form + factor * products[:, q * rows:(q + 1) * rows]
+    cut = width // n_out
+    packed = cut // 2
+    taken = min(packed, 128)
     for c in range(width // 128):
-        hidden_t[c * 128:(c + 1) * 128, :] = jnp.transpose(hidden[:, c * 128:(c + 1) * 128])
+        turned = jnp.transpose(hidden[:, c * 128:(c + 1) * 128])
+        for r in range(0, 128, taken):
+            group, inside = divmod(c * 128 + r, cut)
+            to = group * packed + inside % packed
+            hidden_t[to:to + taken, inside // packed * rows:(inside // packed + 1) * rows] = turned[r:r + taken]
 
     each_far(lambda k, o: far_copy(W_FAR, k, w_far.at[me_out], w_far.at[lax.rem(me_out + n_out - k, n_out)], o).wait_recv())
     w = w_far[...].reshape(width, 2 * state)
@@ -344,6 +352,20 @@
         c_back[t, at, :] = jnp.where(comes_first, by_own, got)
         core_home(way, k, core, t).start()
 
+    def term_copy(way, k, o, source):
+        return far_copy(G_FAR + way, k, g_send.at[way, o], g_recv.at[way, source], o)
+
+    def send_term(way, low):
+        zero = jnp.zeros_like(low)
+        pair = jnp.concatenate(
+            [jnp.concatenate([low, zero], axis=1), jnp.concatenate([zero, low], axis=1)], axis=0
+        )
+        term = (dot(hidden_t[...], pair) * scale).astype(BF16)
+        for o in range(n_out):
+            g_send[way, o] = term[o * packed:(o + 1) * packed]
+        each_far(lambda k, o: term_copy(way, k, o, me_out).start())
+        g_recv[way, me_out] = g_send[way, me_out]
+
     sums = []
     for way, near in enumerate((near_c, near_b)):
         def share_arrived(k, t):
@@ -355,24 +377,20 @@
         each_chip(share_arrived)
         sum_ = use_half(way, core, near)
         each_slice(lambda k, t: core_home(way, k - 1, other, source_of(k - 1)).wait_recv())
-        sums.append(use_half(way, other, sum_))
-    sums = sums[::-1]
-    d_low = jnp.concatenate(sums, axis=1).astype(BF16)
-
-    cut = width // n_out
-    for q in range(2):
-        term = (dot(hidden_t[q * width // 2:(q + 1) * width // 2, :], d_low) * scale).astype(BF16)
-        for o in range(n_out // 2):
-            g_send[q * n_out // 2 + o] = term[o * cut:(o + 1) * cut]
-    each_far(lambda k, o: far_copy(G_FAR, k, g_send.at[o], g_recv.at[me_out], o).start())
-    g_recv[me_out] = g_send[me_out]
+        sums.append(use_half(way, other, sum_).astype(BF16))
+        send_term(way, sums[way])
+    d_low = jnp.concatenate(sums[::-1], axis=1)
 
     gh[...] = dot(d_low, w, NT)
     store_gh = pltpu.make_async_copy(gh, gh_hbm, load_sem.at[0])
     store_gh.start()
 
-    each_far(lambda k, o: far_copy(G_FAR, k, g_send.at[o], g_recv.at[lax.rem(me_out + n_out - k, n_out)], o).wait_recv())
-    g_sum[...] = functools.reduce(lambda a, b: a + b, [g_recv[o].astype(F32) for o in range(n_out)])
+    halves = []
+    for way in range(WAYS):
+        each_far(lambda k, o: term_copy(way, k, o, lax.rem(me_out + n_out - k, n_out)).wait_recv())
+        halves.append(functools.reduce(lambda a, b: a + b, [g_recv[way, o].astype(F32) for o in range(n_out)]))
+    g_sum[:packed] = jnp.concatenate([halves[1][:, :state], halves[0][:, :state]], axis=1)
+    g_sum[packed:] = jnp.concatenate([halves[1][:, state:], halves[0][:, state:]], axis=1)
 
     def owned(i):
         return g_sum.at[pl.ds(pl.multiple_of(i // per_tile * tile, tile), tile), :]
@@ -405,7 +423,8 @@
         each_slice(lambda k, t: core_home(way, k - 1, core, source_of(k - 1)).wait_send())
     each_far(lambda k, o: far_copy(S_FAR, k, o_send.at[o], o_recv.at[me_out], o).wait_send())
     each_far(lambda k, o: far_copy(S_BACK, k, o_back.at[o], carry.at[me_out], o).wait_send())
-    each_far(lambda k, o: far_copy(G_FAR, k, g_send.at[o], g_recv.at[me_out], o).wait_send())
+    for way in range(WAYS):
+        each_far(lambda k, o: term_copy(way, k, o, me_out).wait_send())
     each_near(lambda k, i: near_copy(G_NEAR, k, owned(i), g_near.at[me_in], i).wait_send())
     store_gh.wait()
     store_gx.wait()
@@ -457,7 +476,7 @@
             pltpu.VMEM((rows, lanes), BF16),
             pltpu.VMEM((heads, rows), F32),
             pltpu.VMEM((heads, rows), F32),
-            pltpu.VMEM((width, rows), BF16),
+            pltpu.VMEM((width // 2, 2 * rows), BF16),
             pltpu.VMEM((rows, lanes), F32),
             pltpu.VMEM((rows, width), F32),
             pltpu.VMEM((n_in, tile, columns), F32),
@@ -481,8 +500,8 @@
             pltpu.VMEM((n_in // 2, columns, part), F32),
             pltpu.VMEM((n_in // 2, columns, part), F32),
             pltpu.VMEM((2, n_in // 2, columns, part), F32),
-            pltpu.VMEM((n_out, width // n_out, columns), BF16),
-            pltpu.VMEM((n_out, width // n_out, columns), BF16),
+            pltpu.VMEM((2, n_out, width // n_out // 2, columns), BF16),
+            pltpu.VMEM((2, n_out, width // n_out // 2, columns), BF16),
             pltpu.VMEM((width // n_out, columns), F32),
             pltpu.VMEM((n_in, tile, columns), F32),
             pltpu.SemaphoreType.DMA((5,)),

time: 77.8 us -> 76.9 us (0.988)
  Pallas kernels: 77 us -> 76.1 us
    pallas_call x1, Pallas kernels: 74.8 us -> 73.9 us  [per_device(): pl.pallas_call(functools.partial(kernel, scale, n_out, n_in), out_shape=(...]
where the time goes in v5:
time: 76.9 us; the launch traced here: 76.8 us
  Pallas kernels  76.1 us (99%)
    pallas_call x1, Pallas kernels, per_device(): pl.pallas_call(functools.partial(kernel, scale, n_out, n_in), out_shape=(...  73.9 us
    pallas_call x1, Pallas kernels, per_device(): pl.pallas_call(write_out, out_shape=tuple((jax.ShapeDtypeStruct(r.shape,...  2.25 us

profile of v5, /device:TPU:1, one launch (start us, length us, event | category | flops | bytes accessed | tf_op | source)
XLA Modules:
  0.0 76.8 jit_solution(17961485557988557474)
XLA Ops:
  0.6 73.9 %shard_map.85 = (f32[128,2048]{1,0:T(8,128)}, f32[128,1024]{1,0:T(8,128)}, f32[4,128]{1,0:T(4,128)}) custom-call(bf16[128,1024]{1,0:T(8,128)(2,1)} %hidden_hbm.1, bf16[128,2048]{1,0:T(8,128)(2,1)} %x_hbm.1, f32[32,128]{1,0:T(8,128)} %bitcast.2, f32[32,128]{1,0:T(8,128)} %bitcast.3, bf16[4,128]{1,0:T(4,128)(2,1)} %w_ref.1, bf16[128,2048]{1,0:T(8,128)(2,1)} %gy_hbm.1), custom_call_target="tpu_custom_call" | custom-call | flops 1000000000 | bytes 3000000 | tf_op jit(solution)/shard_map/pallas_call | solution.py:464
  74.5 2.3 %shard_map.86 = (f32[128,2048]{1,0:T(8,128)}, f32[128,1024]{1,0:T(8,128)}, f32[4,128]{1,0:T(4,128)}) custom-call(f32[128,2048]{1,0:T(8,128)} %get-tuple-element.6.gx_from, f32[128,1024]{1,0:T(8,128)} %get-tuple-element.7.gh_from, f32[4,128]{1,0:T(4,128)} %get-tuple-element.8.gp_from), custom_call_target="tpu_custom_call" | custom-call | tf_op jit(solution)/shard_map/pallas_call | solution.py:517

commit v6 on v5

--- a/solution.py
+++ b/solution.py
@@ -385,19 +385,6 @@
     store_gh = pltpu.make_async_copy(gh, gh_hbm, load_sem.at[0])
     store_gh.start()
 
-    halves = []
-    for way in range(WAYS):
-        each_far(lambda k, o: term_copy(way, k, o, lax.rem(me_out + n_out - k, n_out)).wait_recv())
-        halves.append(functools.reduce(lambda a, b: a + b, [g_recv[way, o].astype(F32) for o in range(n_out)]))
-    g_sum[:packed] = jnp.concatenate([halves[1][:, :state], halves[0][:, :state]], axis=1)
-    g_sum[packed:] = jnp.concatenate([halves[1][:, state:], halves[0][:, state:]], axis=1)
-
-    def owned(i):
-        return g_sum.at[pl.ds(pl.multiple_of(i // per_tile * tile, tile), tile), :]
-
-    each_near(lambda k, i: near_copy(G_NEAR, k, owned(i), g_near.at[me_in], i).start())
-    g_near[me_in] = g_sum[pl.ds(pl.multiple_of(me_in // per_tile * tile, tile), tile), :]
-
     b_hi, b_lo = split(b_rows)
     b_three = jnp.concatenate([b_hi, b_lo, b_hi], axis=1)
     for i in range(n_in):
@@ -407,12 +394,18 @@
     store_gx = pltpu.make_async_copy(gx, gx_hbm, load_sem.at[1])
     store_gx.start()
 
-    each_near(lambda k, i: near_copy(G_NEAR, k, owned(i), g_near.at[lax.rem(me_in + n_in - k, n_in)], i).wait_recv())
-    summed = functools.reduce(lambda a, b: a + b, [g_near[i] for i in range(n_in)])
-    mine = summed[:own_rows]
-    for q in range(1, per_tile):
-        mine = jnp.where(lax.rem(me_in, per_tile) == q, summed[q * own_rows:(q + 1) * own_rows], mine)
-    gp_ref[...] = mine
+    halves = []
+    for way in range(WAYS):
+        each_far(lambda k, o: term_copy(way, k, o, lax.rem(me_out + n_out - k, n_out)).wait_recv())
+        halves.append(functools.reduce(lambda a, b: a + b, [g_recv[way, o].astype(F32) for o in range(n_out)]))
+    g_sum[:packed] = jnp.concatenate([halves[1][:, :state], halves[0][:, :state]], axis=1)
+    g_sum[packed:] = jnp.concatenate([halves[1][:, state:], halves[0][:, state:]], axis=1)
+
+    def owned(i):
+        return g_sum.at[pl.ds(pl.multiple_of(i // per_tile * tile, tile), tile), :]
+
+    each_near(lambda k, i: near_copy(G_NEAR, k, owned(i), g_near.at[me_in], i).start())
+    g_near[me_in] = g_sum[pl.ds(pl.multiple_of(me_in // per_tile * tile, tile), tile), :]
 
     each_near(lambda k, i: near_copy(W_NEAR, k, w_near.at[me_in], w_near.at[me_in], i).wait_send())
     each_far(lambda k, o: far_copy(W_FAR, k, w_far.at[me_out], w_far.at[me_out], o).wait_send())
@@ -425,6 +418,13 @@
     each_far(lambda k, o: far_copy(S_BACK, k, o_back.at[o], carry.at[me_out], o).wait_send())
     for way in range(WAYS):
         each_far(lambda k, o: term_copy(way, k, o, me_out).wait_send())
+    each_near(lambda k, i: near_copy(G_NEAR, k, owned(i), g_near.at[lax.rem(me_in + n_in - k, n_in)], i).wait_recv())
+    summed = functools.reduce(lambda a, b: a + b, [g_near[i] for i in range(n_in)])
+    mine = summed[:own_rows]
+    for q in range(1, per_tile):
+        mine = jnp.where(lax.rem(me_in, per_tile) == q, summed[q * own_rows:(q + 1) * own_rows], mine)
+    gp_ref[...] = mine
+
     each_near(lambda k, i: near_copy(G_NEAR, k, owned(i), g_near.at[me_in], i).wait_send())
     store_gh.wait()
     store_gx.wait()

time: 76.9 us -> 75.9 us (0.987)
  Pallas kernels: 76.1 us -> 75.1 us
    pallas_call x1, Pallas kernels: 73.9 us -> 72.8 us  [per_device(): pl.pallas_call(functools.partial(kernel, scale, n_out, n_in), out_shape=(...]
where the time goes in v6:
time: 75.9 us; the launch traced here: 75.7 us
  Pallas kernels  75.1 us (99%)
    pallas_call x1, Pallas kernels, per_device(): pl.pallas_call(functools.partial(kernel, scale, n_out, n_in), out_shape=(...  72.8 us
    pallas_call x1, Pallas kernels, per_device(): pl.pallas_call(write_out, out_shape=tuple((jax.ShapeDtypeStruct(r.shape,...  2.25 us

profile of v6, /device:TPU:1, one launch (start us, length us, event | category | flops | bytes accessed | tf_op | source)
XLA Modules:
  0.0 75.7 jit_solution(10436505897402254968)
XLA Ops:
  0.6 72.8 %shard_map.85 = (f32[128,2048]{1,0:T(8,128)}, f32[128,1024]{1,0:T(8,128)}, f32[4,128]{1,0:T(4,128)}) custom-call(bf16[128,1024]{1,0:T(8,128)(2,1)} %hidden_hbm.1, bf16[128,2048]{1,0:T(8,128)(2,1)} %x_hbm.1, f32[32,128]{1,0:T(8,128)} %bitcast.2, f32[32,128]{1,0:T(8,128)} %bitcast.3, bf16[4,128]{1,0:T(4,128)(2,1)} %w_ref.1, bf16[128,2048]{1,0:T(8,128)(2,1)} %gy_hbm.1), custom_call_target="tpu_custom_call" | custom-call | flops 1000000000 | bytes 3000000 | tf_op jit(solution)/shard_map/pallas_call | solution.py:464
  73.5 2.3 %shard_map.86 = (f32[128,2048]{1,0:T(8,128)}, f32[128,1024]{1,0:T(8,128)}, f32[4,128]{1,0:T(4,128)}) custom-call(f32[128,2048]{1,0:T(8,128)} %get-tuple-element.6.gx_from, f32[128,1024]{1,0:T(8,128)} %get-tuple-element.7.gh_from, f32[4,128]{1,0:T(4,128)} %get-tuple-element.8.gp_from), custom_call_target="tpu_custom_call" | custom-call | tf_op jit(solution)/shard_map/pallas_call | solution.py:517

commit v7 on v6

--- a/solution.py
+++ b/solution.py
@@ -253,8 +253,8 @@
 
     give(0)
     own_half(0, core)
+    join(0)
     give(1)
-    join(0)
     own_half(1, core)
     join(1)
 

time: 75.9 us -> 76.1 us (level)
  no operation moved by 1% of the time
where the time goes in v7:
time: 76.1 us; the launch traced here: 76 us
  Pallas kernels  75.3 us (99%)
    pallas_call x1, Pallas kernels, per_device(): pl.pallas_call(functools.partial(kernel, scale, n_out, n_in), out_shape=(...  73.1 us
    pallas_call x1, Pallas kernels, per_device(): pl.pallas_call(write_out, out_shape=tuple((jax.ShapeDtypeStruct(r.shape,...  2.25 us

profile of v7, /device:TPU:1, one launch (start us, length us, event | category | flops | bytes accessed | tf_op | source)
XLA Modules:
  0.0 76.0 jit_solution(15695386209951683573)
XLA Ops:
  0.6 73.1 %shard_map.85 = (f32[128,2048]{1,0:T(8,128)}, f32[128,1024]{1,0:T(8,128)}, f32[4,128]{1,0:T(4,128)}) custom-call(bf16[128,1024]{1,0:T(8,128)(2,1)} %hidden_hbm.1, bf16[128,2048]{1,0:T(8,128)(2,1)} %x_hbm.1, f32[32,128]{1,0:T(8,128)} %bitcast.2, f32[32,128]{1,0:T(8,128)} %bitcast.3, bf16[4,128]{1,0:T(4,128)(2,1)} %w_ref.1, bf16[128,2048]{1,0:T(8,128)(2,1)} %gy_hbm.1), custom_call_target="tpu_custom_call" | custom-call | flops 1000000000 | bytes 3000000 | tf_op jit(solution)/shard_map/pallas_call | solution.py:464
  73.7 2.3 %shard_map.86 = (f32[128,2048]{1,0:T(8,128)}, f32[128,1024]{1,0:T(8,128)}, f32[4,128]{1,0:T(4,128)}) custom-call(f32[128,2048]{1,0:T(8,128)} %get-tuple-element.6.gx_from, f32[128,1024]{1,0:T(8,128)} %get-tuple-element.7.gh_from, f32[4,128]{1,0:T(4,128)} %get-tuple-element.8.gp_from), custom_call_target="tpu_custom_call" | custom-call | tf_op jit(solution)/shard_map/pallas_call | solution.py:517
